TPU v7x, 512 devices: a whole 4x4x16 slice. The times are simulated.
512 devices in a mesh: crop: 16 (over x, y_lo, core), dap: 32 (over y_hi, z).
Axes of the slice: x: 4, y: 4 (y_hi: 2, y_lo: 2; y = y_hi * 2 + y_lo), z: 16, core: 2. Of those that a mesh axis runs over, the one named last changes fastest.
Arguments:
- pair: float32 [16, 128, 128, 128], P('crop', 'dap'), may hold values from -6 to 6
- pair_grad: float32 [16, 128, 128, 128], P('crop', 'dap'), may hold values from -6 to 6
- norm_gain: float32 [2, 128], replicated, may hold values from 0.5 to 1.5
- norm_shift: float32 [2, 128], replicated, may hold values from -3 to 3
- proj_weight: float32 [2, 4, 128, 128], replicated, may hold values from -0.5 to 0.5
- bias_weight: float32 [2, 4, 128], replicated, may hold values from -0.5 to 0.5
- gate_shift: float32 [2, 128], replicated, may hold values from -4 to 4
- out_weight: float32 [2, 128, 128], replicated, may hold values from -0.5 to 0.5
- out_shift: float32 [2, 128], replicated, may hold values from -3 to 3
Outputs:
- new_pair: float32 [16, 128, 128, 128], P('crop', 'dap')
- input_grad: float32 [16, 128, 128, 128], P('crop', 'dap')
- grad_gain: float32 [2, 128], replicated
- grad_shift: float32 [2, 128], replicated
- grad_proj: float32 [2, 4, 128, 128], replicated
- grad_bias: float32 [2, 4, 128], replicated
- grad_gate: float32 [2, 128], replicated
- grad_out: float32 [2, 128, 128], replicated
- grad_outshift: float32 [2, 128], replicated
All inputs are finite; a program needn't handle non-finite values.
Results may differ from a plain program's by a relative error of at most 0.00011.
Values sent between devices are 32-bit elements; how exact they have to be, the bound alone decides.
A program may use at most 64 MiB of HBM per device.

v0:
```python
import jax
import jax.numpy as jnp
from jax import lax
from jax.sharding import PartitionSpec as P

HEADS = 4


EPSILON = 1e-05
HIGHEST = lax.Precision.HIGHEST


def layer_norm(field, gain, shift):
    center = field - jnp.mean(field, axis=-1, keepdims=True)
    spread = jnp.mean(center * center, axis=-1, keepdims=True)
    return center * lax.rsqrt(spread + EPSILON) * gain + shift


def project(pair_rows, gain, shift, weights, bias_proj):
    normed = layer_norm(pair_rows, gain, shift)
    stacked = jnp.einsum("ijc,gcd->gijd", normed, weights, precision=HIGHEST)
    bias_rows = jnp.einsum("ijc,hc->hij", normed, bias_proj, precision=HIGHEST)
    return (stacked, bias_rows)


def attend(stacked, bias_full, gate_bias, out_proj, out_bias):
    row_count, col_count, channels = (stacked.shape[1], stacked.shape[2], stacked.shape[3])
    head_size = channels // HEADS
    shape = (row_count, col_count, HEADS, head_size)
    queries = stacked[0].reshape(shape) * head_size ** (-0.5)
    key_rows = stacked[1].reshape(shape)
    value_rows = stacked[2].reshape(shape)
    scores = jnp.einsum("ijhd,ikhd->ihjk", queries, key_rows, precision=HIGHEST) + bias_full[None]
    probs = jax.nn.softmax(scores, axis=-1)
    attended = jnp.einsum("ihjk,ikhd->ijhd", probs, value_rows, precision=HIGHEST).reshape(
        row_count, col_count, channels
    )
    gated_out = jax.nn.sigmoid(stacked[3] + gate_bias) * attended
    return jnp.einsum("ijc,cd->ijd", gated_out, out_proj, precision=HIGHEST) + out_bias


def block_forward(pair_rows, params):
    stacked, bias_rows = project(pair_rows, *params[:4])
    bias_full = lax.all_gather(bias_rows, "dap", axis=1, tiled=True)
    change = attend(stacked, bias_full, *params[4:])
    return (change, bias_full)


def block_backward(cotangent, pair_rows, bias_full, params):
    (stacked, unused_rows), back_first = jax.vjp(project, pair_rows, *params[:4])
    unused_change, back_second = jax.vjp(attend, stacked, bias_full, *params[4:])
    grads_second = back_second(cotangent)
    d_stacked, d_bias_full = (grads_second[0], grads_second[1])
    summed = lax.psum(d_bias_full, "dap")
    row_count = cotangent.shape[0]
    d_bias_rows = lax.dynamic_slice_in_dim(summed, lax.axis_index("dap") * row_count, row_count, 1)
    grads_first = back_first((d_stacked, d_bias_rows))
    return (grads_first[0], tuple(grads_first[1:]) + tuple(grads_second[2:]))


def body(
    pair,
    pair_grad,
    norm_gain,
    norm_shift,
    proj_weight,
    bias_weight,
    gate_shift,
    out_weight,
    out_shift,
):
    start_rows = pair[0]
    upstream = pair_grad[0]
    params_all = (
        norm_gain,
        norm_shift,
        proj_weight,
        bias_weight,
        gate_shift,
        out_weight,
        out_shift,
    )
    start_params = tuple((member[0] for member in params_all))
    end_params = tuple((member[1] for member in params_all))
    change_start, bias_start = block_forward(start_rows, start_params)
    middle_rows = start_rows + change_start
    middle_cols = lax.all_to_all(middle_rows, "dap", split_axis=1, concat_axis=0, tiled=True)
    end_rows = jnp.swapaxes(middle_cols, 0, 1)
    change_end, bias_end = block_forward(end_rows, end_params)
    change_back = lax.all_to_all(
        jnp.swapaxes(change_end, 0, 1), "dap", split_axis=0, concat_axis=1, tiled=True
    )
    upstream_cols = lax.all_to_all(upstream, "dap", split_axis=1, concat_axis=0, tiled=True)
    delta_cols, grads_end = block_backward(
        jnp.swapaxes(upstream_cols, 0, 1), end_rows, bias_end, end_params
    )
    delta_rows = lax.all_to_all(
        jnp.swapaxes(delta_cols, 0, 1), "dap", split_axis=0, concat_axis=1, tiled=True
    )
    new_rows = middle_rows + change_back
    middle_grad = upstream + delta_rows
    delta_start, grads_start = block_backward(middle_grad, start_rows, bias_start, start_params)
    input_rows = middle_grad + delta_start
    scale = 1.0 / (lax.axis_size("crop") * pair.shape[2])
    stacked_grads = tuple(
        (
            jnp.stack([first_part, second_part]) * scale
            for first_part, second_part in zip(grads_start, grads_end)
        )
    )
    totals = lax.psum(stacked_grads, ("crop", "dap"))
    return (
        new_rows[None],
        input_rows[None],
        totals[0],
        totals[1],
        totals[2],
        totals[3],
        totals[4],
        totals[5],
        totals[6],
    )


def solution(mesh):
    return jax.shard_map(
        body,
        mesh=mesh,
        in_specs=(
            P("crop", "dap", None, None),
            P("crop", "dap", None, None),
            P(),
            P(),
            P(),
            P(),
            P(),
            P(),
            P(),
        ),
        out_specs=(
            P("crop", "dap", None, None),
            P("crop", "dap", None, None),
            P(),
            P(),
            P(),
            P(),
            P(),
            P(),
            P(),
        ),
        check_vma=False,
    )
```

profile of v0, /device:TPU:1, one launch (start us, length us, event | category | flops | bytes accessed | tf_op | source)
XLA Modules:
  0.0 1343.7 jit_solution(12001489790199699557)
XLA Ops:
  12.9 70.8 %all_gather.6 = f32[4,128,128]{2,0,1:T(4,128)S(1)} all-gather(f32[4,4,128]{2,0,1:T(4,128)S(1)} %convolution_bitcast_fusion.9), channel_id=1, replica_groups=mesh['crop'=16,'dap'=32] {'dap'}, dimensions={1}, use_global_device_ids=true | all-gather | bytes 270336 | tf_op jit(solution)/shard_map/all_gather | solution.py:44
  85.2 1.8 fusion.110
  87.3 1.8 bitcast_multiply_fusion.5
  90.7 4.0 all-to-all-start
  95.7 17.6 %all-to-all-done = f32[4,128,128]{2,0,1:T(4,128)S(1)} async-done(((f32[4,128,128]{2,0,1:T(4,128)}), f32[4,128,128]{2,0,1:T(4,128)S(1)}, u32[]{:S(2)}, u32[]{:S(2)}) %all-to-all-start) | async-done | bytes 262176 | tf_op jit(solution)/shard_map/all_to_all | solution.py:87
  114.0 3.9 all-to-all-start.2
  121.1 2.1 convolution_bitcast_fusion
  123.2 13.3 all-to-all-done.2
  137.3 64.2 %all_gather.7 = f32[4,128,128]{2,0,1:T(4,128)} all-gather(f32[4,4,128]{2,0,1:T(4,128)S(1)} %convolution_bitcast_fusion.8), channel_id=1, replica_groups=mesh['crop'=16,'dap'=32] {'dap'}, dimensions={1}, use_global_device_ids=true | all-gather | bytes 270336 | tf_op jit(solution)/shard_map/all_gather | solution.py:44
  201.4 1.8 copy.50
  204.5 1.8 fusion.111
  206.6 1.8 bitcast_multiply_fusion.4
  208.4 2.7 fusion.104
  211.1 2.5 fusion.10
  213.5 1.9 multiply_reduce_fusion.1
  216.4 2.4 fusion.112
  220.6 1.8 copy.57
  225.7 4.8 all-to-all-start.1
  230.5 3.8 convolution_bitcast_fusion.5
  234.3 285.6 %all-reduce.14.cloned.1.call-done = f32[4,128,128]{2,0,1:T(4,128)} async-done(((f32[4,128,128]{2,0,1:T(4,128)}), f32[4,128,128]{2,0,1:T(4,128)}) %all-reduce.14.cloned.1.call-update) | async-done | bytes 262160 | tf_op jit(solution)/shard_map/psum | solution.py:54
  519.9 2.2 fusion.101
  524.9 5.9 all-to-all-start.3
  532.1 2.3 convolution_bitcast_fusion.2
  538.3 11.1 all-to-all-done.3
  552.7 2.5 fusion.14
  555.1 1.8 multiply_reduce_fusion
  557.9 1.7 fusion.113
  565.8 1.8 convolution_bitcast_fusion.4
  567.7 282.7 %all-reduce.16.cloned.1.call-done = f32[4,128,128]{2,0,1:T(4,128)} async-done(((f32[4,128,128]{2,0,1:T(4,128)}), f32[4,128,128]{2,0,1:T(4,128)}) %all-reduce.16.cloned.1.call-update) | async-done | bytes 262160 | tf_op jit(solution)/shard_map/psum | solution.py:54
  856.3 122.0 %all-reduce.8 = (f32[2,128]{1,0:T(2,128)}, f32[2,128]{1,0:T(2,128)}, f32[2,4,128]{2,1,0:T(4,128)}, f32[2,128]{1,0:T(2,128)}, f32[2,128]{1,0:T(2,128)}) all-reduce(f32[2,128]{1,0:T(2,128)S(1)} %maximum_multiply_fusion.3, f32[2,128]{1,0:T(2,128)S(1)} %maximum_multiply_fusion.4, ...), channel_id=1, replica_groups=mesh['crop'=16,'dap'=32] {'crop','dap'}, use_global_device_ids=true, to_apply=%region_20.0 | all-reduce | flops 2048 | bytes 16384 | tf_op jit(solution)/shard_map/psum | solution.py:111
  978.3 355.9 %all-reduce.18.cloned.1.call-done = (f32[2,4,128,128]{2,3,1,0:T(8,128)}, f32[2,128,128]{2,1,0:T(8,128)}) async-done(((f32[2,4,128,128]{2,3,1,0:T(8,128)}, f32[2,128,128]{2,1,0:T(8,128)}), (f32[2,4,128,128]{2,3,1,0:T(8,128)}, f32[2,128,128]{2,1,0:T(8,128)})) %all-reduce.18.cloned.1.call-update) | async-done | bytes 655376 | tf_op jit(solution)/shard_map/psum | solution.py:111
  1334.2 2.1 copy.71
  (193 shorter events, 46.7 us)
Async XLA Ops:
  7.2 2.4 copy-start
  10.5 73.4 %copy-start.26 = (f32[4,128]{1,0:T(4,128)}, f32[4,128]{1,0:T(4,128)S(1)}, u32[]{:S(2)}) copy-start(f32[4,128]{1,0:T(4,128)S(1)} %fusion.87) | copy-start | bytes 6148
  11.7 72.2 %copy-start.35 = (f32[128]{0:T(128)}, f32[128]{0:T(128)S(1)}, u32[]{:S(2)}) copy-start(f32[128]{0:T(128)S(1)} %get-tuple-element.93) | copy-start | bytes 1540
  11.7 72.2 %copy-start.44 = (f32[128]{0:T(128)}, f32[128]{0:T(128)S(1)}, u32[]{:S(2)}) copy-start(f32[128]{0:T(128)S(1)} %get-tuple-element.78) | copy-start | bytes 1540
  11.7 109.3 %copy-start.37 = (f32[128]{0:T(128)}, f32[128]{0:T(128)S(1)}, u32[]{:S(2)}) copy-start(f32[128]{0:T(128)S(1)} %get-tuple-element.94) | copy-start | bytes 1540
  11.8 109.3 %copy-start.46 = (f32[128]{0:T(128)}, f32[128]{0:T(128)S(1)}, u32[]{:S(2)}) copy-start(f32[128]{0:T(128)S(1)} %get-tuple-element.77) | copy-start | bytes 1540
  12.4 71.5 %copy-start.14 = (f32[2,4,128,128]{3,2,1,0:T(8,128)S(1)}, f32[2,4,128,128]{3,2,1,0:T(8,128)}, u32[]{:S(2)}) copy-start(f32[2,4,128,128]{3,2,1,0:T(8,128)} %param.13) | copy-start | bytes 1572868
  85.2 1.9 copy-start.2
  85.2 1.9 copy-start.4
  85.2 2.0 copy-start.12
  87.2 1.8 copy-start.23
  90.7 4.1 copy-start.1
  90.7 22.6 %all-to-all-start = ((f32[4,128,128]{2,0,1:T(4,128)}), f32[4,128,128]{2,0,1:T(4,128)S(1)}, u32[]{:S(2)}, u32[]{:S(2)}) async-start(f32[4,128,128]{2,0,1:T(4,128)} %copy.47), calls=%async_computation | async-start | bytes 524288 | tf_op jit(solution)/shard_map/all_to_all | solution.py:87
  114.0 22.5 %all-to-all-start.2 = ((f32[4,128,128]{2,0,1:T(4,128)}), f32[4,128,128]{2,0,1:T(4,128)S(1)}, u32[]{:S(2)}, u32[]{:S(2)}) async-start(f32[4,128,128]{2,0,1:T(4,128)} %copy.55), calls=%async_computation.2 | async-start | bytes 524288 | tf_op jit(solution)/shard_map/all_to_all | solution.py:93
  117.9 402.0 %all-reduce.14.cloned.1.call-start = ((), (), s32[]{:S(2)}) async-start(), calls=%async_computation.4 | async-start | bytes 524288 | tf_op jit(solution)/shard_map/psum | solution.py:54
  119.1 2.0 copy-start.15
  225.7 299.1 %all-to-all-start.1 = ((f32[128,4,128]{2,1,0:T(4,128)}), f32[128,4,128]{2,1,0:T(4,128)}, u32[]{:S(2)}, u32[]{:S(2)}) async-start(f32[128,4,128]{2,1,0:T(4,128)} %copy.53), calls=%async_computation.1 | async-start | bytes 524288 | tf_op jit(solution)/shard_map/all_to_all | solution.py:90
  230.5 289.4 %copy-start.38 = (f32[128]{0:T(128)S(1)}, f32[128]{0:T(128)}, u32[]{:S(2)}) copy-start(f32[128]{0:T(128)} %copy-done.37) | copy-start | bytes 1540
  230.5 289.4 %copy-start.41 = (f32[2,4,128]{2,1,0:T(4,128)S(1)}, f32[2,4,128]{2,1,0:T(4,128)}, u32[]{:S(2)}) copy-start(f32[2,4,128]{2,1,0:T(4,128)} %param.14) | copy-start | bytes 12292
  519.9 2.2 copy-start.30
  519.9 2.2 copy-start.32
  524.9 5.9 copy-start.24
  524.9 24.5 %all-to-all-start.3 = ((f32[128,4,128]{2,1,0:T(4,128)}), f32[128,4,128]{2,1,0:T(4,128)}, u32[]{:S(2)}, u32[]{:S(2)}) async-start(f32[128,4,128]{2,1,0:T(4,128)} %copy.63), calls=%async_computation.3 | async-start | bytes 524288 | tf_op jit(solution)/shard_map/all_to_all | solution.py:97
  530.7 319.6 %all-reduce.16.cloned.1.call-start = ((), (), s32[]{:S(2)}) async-start(), calls=%async_computation.5 | async-start | bytes 524288 | tf_op jit(solution)/shard_map/psum | solution.py:54
  532.1 2.3 copy-start.10
  532.1 2.4 copy-start.17
  552.7 2.5 copy-start.13
  552.7 2.5 copy-start.28
  561.6 772.6 %all-reduce.18.cloned.1.call-start = ((), (), s32[]{:S(2)}) async-start(), calls=%async_computation.6 | async-start | bytes 1310720 | tf_op jit(solution)/shard_map/psum | solution.py:111
  567.6 282.8 %copy-start.42 = (f32[2,4,128]{2,1,0:T(4,128)S(1)}, f32[2,4,128]{2,1,0:T(4,128)}, u32[]{:S(2)}) copy-start(f32[2,4,128]{2,1,0:T(4,128)} %param.14) | copy-start | bytes 12292
  567.6 284.1 %copy-start.34 = (f32[4,128]{1,0:T(4,128)S(1)}, f32[4,128]{1,0:T(4,128)}, u32[]{:S(2)}) copy-start(f32[4,128]{1,0:T(4,128)} %copy-done.33) | copy-start | bytes 6148
  1334.2 2.1 copy-start.18
  (35 other events, 32.7 us)
Sparse Core Ops, SparseCore 0:
  222.6 297.3 all-reduce.13
  561.7 288.6 all-reduce.15
  856.4 477.7 all-reduce.17
where the time goes:
time: 1350 us; the launch traced here: 1340 us
  waiting for transfers between devices  966 us (72%)
  blocking collectives  257 us (19%)
  matrix products  49.2 us (4%)
  local copies, waits for them, and re-layouts  26.3 us (2%)
  starting transfers between devices  18.8 us (1%)
  between operations  14.6 us (1%)
    psum x2, waiting for transfers between devices, block_backward(): summed = lax.psum(d_bias_full, 'dap')  568 us
    psum x1, waiting for transfers between devices, body(): totals = lax.psum(stacked_grads, ('crop', 'dap'))  356 us
    all_gather x2, blocking collectives, block_forward(): bias_full = lax.all_gather(bias_rows, 'dap', axis=1, tiled=True)  135 us
    psum x1, blocking collectives, body(): totals = lax.psum(stacked_grads, ('crop', 'dap'))  122 us
  transfers between devices with their start and end apart: 7, of which 6 were waited for; matrix products, arithmetic and copies ran while one was open for 2% of the time, Pallas kernels for 0%

commit v1 on v0

v1 whole, which is shorter than its diff:
```python
import functools

import jax
import jax.numpy as jnp
from jax import lax
from jax.experimental import pallas as pl
from jax.experimental.pallas import tpu as pltpu
from jax.sharding import PartitionSpec as P

HEADS = 4
EPSILON = 1e-05
F32 = jnp.float32
BF16 = jnp.bfloat16
MESH = pl.DeviceIdType.MESH
NN = (((1,), (0,)), ((), ()))
NT = (((1,), (1,)), ((), ()))
Z = 16


def split(x):
    hi = x.astype(BF16)
    return hi, (x - hi.astype(F32)).astype(BF16)


def dot(a, b, dims):
    return lax.dot_general(a, b, dims, preferred_element_type=F32)


def dot3(a, b, dims):
    return dot(a[0], b[0], dims) + (dot(a[0], b[1], dims) + dot(a[1], b[0], dims))


def dot3m(a, b, dims):
    rows = a[0].shape[0]
    both = dot(jnp.concatenate(a, axis=0), b[0], dims)
    return both[:rows] + (both[rows:] + dot(a[0], b[1], dims))


def dot_tn(a, b):
    ah, al = split(a)
    bh, bl = split(b)
    stacked = jnp.concatenate([ah.astype(F32), ah.astype(F32), al.astype(F32), al.astype(F32)], axis=0)
    return dot(stacked.T.astype(BF16), jnp.concatenate([bh, bl, bh, bl], axis=0), NN)


def normalise(z):
    center = z - jnp.mean(z, axis=-1, keepdims=True)
    spread = jnp.mean(center * center, axis=-1, keepdims=True)
    r = lax.rsqrt(spread + EPSILON)
    return center * r, r


def normalise_back(dn, n, r):
    first = jnp.mean(dn, axis=-1, keepdims=True)
    second = jnp.mean(dn * n, axis=-1, keepdims=True)
    return r * (dn - first - n * second)


def kernel(
    D,
    NC,
    pair_ref, grad_ref, gain_ref, shift_ref, w_ref, bw_ref, gs_ref, wo_ref, os_ref,
    new_ref, igrad_ref, ggain_ref, gshift_ref, gproj_ref, gbias_ref, ggate_ref, gout_ref, gos_ref,
    z_ref, n_ref, r_ref, nm_ref, rm_ref, up_ref, mg_ref, dxt_ref,
    wt_ref, xt_ref, pt_ref, at_ref, ot_ref, yt_ref, dot_ref, dpt_ref, bt_ref, db_ref,
    stage_ref, chunk_ref, recv_ref,
    big_ref, bigr_ref, msg_ref, near_ref, far_ref, last_ref, tiny_ref,
    send_sem, recv_sem, wsend_sem, wrecv_sem,
):
    R = 4
    N = R * D
    T = R * N
    C = 128
    HS = C // HEADS
    scale = HS ** (-0.5)
    out_scale = 1.0 / (NC * N)
    me = lax.axis_index("dap")
    crop = lax.axis_index("crop")
    Y = D // Z if D >= Z else 1
    z_len = D // Y
    y_at, z_at = me // z_len, lax.rem(me, z_len)
    near_len, far_len = 4 * Y, z_len // 4
    block, inner = z_at // 4, lax.rem(z_at, 4)
    near_me = y_at * 4 + inner

    barrier = pltpu.get_barrier_semaphore()

    @pl.loop(1, D)
    def _(s):
        pl.semaphore_signal(barrier, inc=1, device_id=(crop, lax.rem(me + s, D)), device_id_type=MESH)

    @pl.loop(1, NC)
    def _(s):
        pl.semaphore_signal(barrier, inc=1, device_id=(lax.rem(crop + s, NC), me), device_id_type=MESH)

    def copy_to(src, dst, sems, k, device):
        return pltpu.make_async_remote_copy(
            src_ref=src, dst_ref=dst, send_sem=sems[0].at[k], recv_sem=sems[1].at[k],
            device_id=device, device_id_type=MESH)

    dap_sems = (send_sem, recv_sem)
    w_sems = (wsend_sem, wrecv_sem)

    def send_all(k, slot):
        @pl.loop(1, D)
        def _(s):
            peer = lax.rem(me + s, D)
            copy_to(stage_ref.at[slot, peer], recv_ref.at[k, me], dap_sems, k, (crop, peer)).start()
        recv_ref[k, me] = stage_ref[slot, me]

    def send_same(k, slot):
        @pl.loop(1, D)
        def _(s):
            peer = lax.rem(me + s, D)
            copy_to(chunk_ref.at[slot], recv_ref.at[k, me], dap_sems, k, (crop, peer)).start()
        recv_ref[k, me] = chunk_ref[slot]

    def wait_bytes(ref, sem):
        pltpu.make_async_copy(ref, ref, sem).wait()

    def arrived(k):
        wait_bytes(recv_ref.at[k, pl.ds(0, D - 1)], recv_sem.at[k])

    def put_stage(slot, row, tile):
        stage_ref[slot, :, row, :] = tile

    def get_recv(k, row):
        return recv_ref[k, :, row, :]

    for i in range(R):
        for j in range(R):
            at = (i * R + j) * D
            z_ref[0, at:at + D] = pair_ref[pl.ds(i * N + j, D, stride=R)]
            tile = grad_ref[pl.ds(i * N + j, D, stride=R)]
            up_ref[at:at + D] = tile
            put_stage(0, i * R + j, tile)

    def prepare(b):
        for g in range(4):
            w = w_ref[b, g]
            if g == 0:
                w = w * scale
            hi, lo = split(w.T)
            wt_ref[b, 0, g * C:(g + 1) * C] = hi
            wt_ref[b, 1, g * C:(g + 1) * C] = lo

    def columns(b):
        rows = jnp.concatenate([gs_ref[b:b + 1], jnp.zeros((7, C), F32)], axis=0)
        return rows.T[:, 0:1]

    def bias_rows(b, x_split):
        bw = jnp.concatenate([bw_ref[b], jnp.zeros((4, C), F32)], axis=0)
        return dot3m(split(bw), x_split, NN)

    def put_chunk(slot, rows):
        for i in range(R):
            chunk_ref[slot, i * HEADS:(i + 1) * HEADS] = rows[0:HEADS, i * N:(i + 1) * N]

    def project(b, x_split):
        out = dot3((wt_ref[b, 0], wt_ref[b, 1]), x_split, NN)
        out_gate = jax.nn.sigmoid(out[3 * C:] + columns(b))
        for i in range(R):
            pt_ref[b, i, 0:3 * C] = out[0:3 * C, i * N:(i + 1) * N]
            pt_ref[b, i, 3 * C:] = out_gate[:, i * N:(i + 1) * N]

    def attend(b):
        @pl.loop(0, R)
        def _(i):
            for h in range(HEADS):
                at = h * HS
                q = pt_ref[b, i, at:at + HS]
                k = pt_ref[b, i, C + at:C + at + HS]
                v = pt_ref[b, i, 2 * C + at:2 * C + at + HS]
                s = dot_tn(k, q) + bt_ref[b, h]
                e = jnp.exp(s - jnp.max(s, axis=0, keepdims=True))
                a = e * (1.0 / jnp.sum(e, axis=0, keepdims=True))
                at_ref[b, i, h] = a
                o = dot3m(split(v), split(a), NN)
                ot_ref[b, i, at:at + HS] = o
                yt_ref[b, i, at:at + HS] = o * pt_ref[b, i, 3 * C + at:3 * C + at + HS]

    def over_rows(ref, b):
        return jnp.concatenate([ref[b, i] for i in range(R)], axis=1)

    def update(b):
        y = split(over_rows(yt_ref, b))
        ut = dot3(split(wo_ref[b].T), y, NN)
        return ut.T + os_ref[b:b + 1]

    def backward(b, du, put_bias_grad):
        du_split = split(du)
        dyt = dot3(split(wo_ref[b]), du_split, NT)
        for i in range(R):
            dy = dyt[:, i * N:(i + 1) * N]
            gate = pt_ref[b, i, 3 * C:]
            dot_ref[i] = dy * gate
            dpt_ref[b, i, 3 * C:] = dy * ot_ref[b, i] * (gate * (1.0 - gate))
        db_ref[b] = jnp.zeros((HEADS, N, N), F32)

        @pl.loop(0, R)
        def _(i):
            for h in range(HEADS):
                at = h * HS
                q = pt_ref[b, i, at:at + HS]
                k = pt_ref[b, i, C + at:C + at + HS]
                v = pt_ref[b, i, 2 * C + at:2 * C + at + HS]
                a = at_ref[b, i, h]
                do = dot_ref[i, at:at + HS]
                row = jnp.sum(do * ot_ref[b, i, at:at + HS], axis=0, keepdims=True)
                ds = a * (dot_tn(v, do) - row)
                db_ref[b, h] += ds
                ds_split = split(ds)
                dpt_ref[b, i, at:at + HS] = dot3m(split(k), ds_split, NN)
                dpt_ref[b, i, C + at:C + at + HS] = dot3m(split(q), ds_split, NT)
                dpt_ref[b, i, 2 * C + at:2 * C + at + HS] = dot3m(split(do), split(a), NT)
        put_bias_grad()
        return du_split

    def dx_local(b):
        total = None
        for g in range(4):
            w = w_ref[b, g]
            if g == 0:
                w = w * scale
            d = jnp.concatenate([dpt_ref[b, i, g * C:(g + 1) * C] for i in range(R)], axis=1)
            term = dot3(split(w), split(d), NN)
            total = term if total is None else total + term
        return total

    def big_grads(b, x_split, du_split):
        rows = 5 * C // NC
        parts = []
        for g in range(4):
            d = jnp.concatenate([dpt_ref[b, i, g * C:(g + 1) * C] for i in range(R)], axis=1)
            out = dot3(x_split, split(d), NT)
            parts.append(out * scale if g == 0 else out)
        parts.append(dot3(split(over_rows(yt_ref, b)), du_split, NN))
        whole = jnp.concatenate(parts, axis=0)
        for p in range(NC):
            big_ref[b, p] = whole[p * rows:(p + 1) * rows]

    def send_big(b):
        @pl.loop(1, NC)
        def _(s):
            peer = lax.rem(crop + s, NC)
            copy_to(big_ref.at[b, peer], bigr_ref.at[b, crop], w_sems, 4 * b, (peer, me)).start()
        bigr_ref[b, crop] = big_ref[b, crop]

    def send_near(b):
        wait_bytes(bigr_ref.at[b, pl.ds(0, NC - 1)], wrecv_sem.at[4 * b])
        rows = 5 * C // NC
        total = bigr_ref[b, 0]
        for p in range(1, NC):
            total = total + bigr_ref[b, p]
        msg_ref[b, 0, 0:rows] = total
        msg_ref[b, 0, rows:rows + 8] = tiny_ref[b]

        @pl.loop(1, near_len)
        def _(s):
            m = lax.rem(near_me + s, near_len)
            peer = (m // 4) * z_len + block * 4 + lax.rem(m, 4)
            copy_to(msg_ref.at[b, 0], near_ref.at[b, near_me], w_sems, 4 * b + 1, (crop, peer)).start()
        near_ref[b, near_me] = msg_ref[b, 0]

    def send_far(b):
        wait_bytes(near_ref.at[b, pl.ds(0, near_len - 1)], wrecv_sem.at[4 * b + 1])
        total = near_ref[b, 0]
        for p in range(1, near_len):
            total = total + near_ref[b, p]
        msg_ref[b, 1] = total

        @pl.loop(1, far_len)
        def _(s):
            m = lax.rem(block + s, far_len)
            peer = y_at * z_len + m * 4 + inner
            copy_to(msg_ref.at[b, 1], far_ref.at[b, block], w_sems, 4 * b + 2, (crop, peer)).start()
        far_ref[b, block] = msg_ref[b, 1]

    def send_last(b):
        wait_bytes(far_ref.at[b, pl.ds(0, far_len - 1)], wrecv_sem.at[4 * b + 2])
        total = far_ref[b, 0]
        for p in range(1, far_len):
            total = total + far_ref[b, p]
        msg_ref[b, 2] = total * out_scale

        @pl.loop(1, NC)
        def _(s):
            peer = lax.rem(crop + s, NC)
            copy_to(msg_ref.at[b, 2], last_ref.at[b, crop], w_sems, 4 * b + 3, (peer, me)).start()
        last_ref[b, crop] = msg_ref[b, 2]

    def finish_big(b):
        wait_bytes(last_ref.at[b, pl.ds(0, NC - 1)], wrecv_sem.at[4 * b + 3])
        rows = 5 * C // NC
        for p in range(NC):
            first = p * rows
            while first < (p + 1) * rows:
                g, at = first // C, first % C
                count = min((p + 1) * rows - first, C - at)
                piece = last_ref[b, p, first - p * rows:first - p * rows + count]
                if g < 4:
                    gproj_ref[b, g, at:at + count] = piece
                else:
                    gout_ref[b, at:at + count] = piece
                first += count
        tiny = last_ref[b, 0, rows:rows + 8]
        for p in range(1, NC):
            tiny = tiny + last_ref[b, p, rows:rows + 8]
        ggain_ref[b:b + 1] = tiny[0:1]
        gshift_ref[b:b + 1] = tiny[1:2]
        gbias_ref[b] = tiny[2:2 + HEADS]
        ggate_ref[b:b + 1] = tiny[6:7]
        gos_ref[b:b + 1] = tiny[7:8]

    def gate_grad(b):
        total = None
        for i in range(R):
            d = dpt_ref[b, i, 3 * C:]
            total = d if total is None else total + d
        return jnp.sum(total.T, axis=0, keepdims=True)

    def bias_grad(k):
        total = recv_ref[k, 0]
        for p in range(1, D):
            total = total + recv_ref[k, p]
        rows = jnp.concatenate([total[i * HEADS:(i + 1) * HEADS] for i in range(R)], axis=1)
        return jnp.concatenate([rows, jnp.zeros((4, T), F32)], axis=0)

    def bias_part(b, dbr, x_split):
        bw = jnp.concatenate([bw_ref[b], jnp.zeros((4, C), F32)], axis=0)
        d_split = split(dbr)
        dxt = dot3(split(bw.T), d_split, NN)
        dbw = dot3m(d_split, x_split, NT)
        return dxt, dbw[0:HEADS]

    def col_sum(x):
        return jnp.sum(x, axis=0, keepdims=True)

    n0, r0 = normalise(z_ref[0])
    n_ref[0] = n0
    r_ref[0] = r0
    x0_split = split((n0 * gain_ref[0:1] + shift_ref[0:1]).T)
    xt_ref[0, 0] = x0_split[0]
    xt_ref[0, 1] = x0_split[1]
    put_chunk(0, bias_rows(0, x0_split))
    pl.semaphore_wait(barrier, D - 1 + NC - 1)
    send_same(0, 0)
    send_all(1, 0)
    prepare(0)
    prepare(1)
    project(0, x0_split)
    arrived(0)
    for h in range(HEADS):
        bt_ref[0, h] = jnp.concatenate([get_recv(0, i * HEADS + h) for i in range(R)], axis=0).T
    attend(0)
    z_ref[1] = z_ref[0] + update(0)

    for row in range(R * R):
        put_stage(1, row, z_ref[1, row * D:(row + 1) * D])
    send_all(2, 1)
    nm, rm = normalise(z_ref[1])
    nm_ref[...] = nm
    rm_ref[...] = rm
    xm_split = split((nm * gain_ref[1:2] + shift_ref[1:2]).T)
    xt_ref[2, 0] = xm_split[0]
    xt_ref[2, 1] = xm_split[1]
    put_chunk(1, bias_rows(1, xm_split))
    send_same(3, 1)

    arrived(2)

    def columns_layout(k):
        return jnp.concatenate([get_recv(k, i * R + j) for j in range(R) for i in range(R)], axis=0)

    n1, r1 = normalise(columns_layout(2))
    n_ref[1] = n1
    r_ref[1] = r1
    x1_split = split((n1 * gain_ref[1:2] + shift_ref[1:2]).T)
    xt_ref[1, 0] = x1_split[0]
    xt_ref[1, 1] = x1_split[1]
    project(1, x1_split)
    arrived(3)
    for h in range(HEADS):
        bt_ref[1, h] = jnp.concatenate([get_recv(3, i * HEADS + h) for i in range(R)], axis=0)
    attend(1)
    u1 = update(1)

    def stage_back(slot, value):
        for j in range(R):
            for i in range(R):
                at = (j * R + i) * D
                put_stage(slot, i * R + j, value[at:at + D])

    stage_back(2, u1)

    arrived(1)
    du1 = columns_layout(1)

    def bias_grad_1():
        for h in range(HEADS):
            for i in range(R):
                put_stage(3, i * HEADS + h, db_ref[1, h, i * D:(i + 1) * D])
        send_all(5, 3)

    du1_split = backward(1, du1, bias_grad_1)
    dx1 = dx_local(1).T
    stage_back(4, normalise_back(dx1 * gain_ref[1:2], n_ref[1], r_ref[1]))
    send_all(6, 4)
    send_all(4, 2)
    big_grads(1, (xt_ref[1, 0], xt_ref[1, 1]), du1_split)
    send_big(1)
    tiny_ref[1, 0:1] = col_sum(dx1 * n_ref[1])
    tiny_ref[1, 1:2] = col_sum(dx1)
    tiny_ref[1, 6:7] = gate_grad(1)
    tiny_ref[1, 7:8] = col_sum(du1)
    arrived(5)
    dxm_t, dbw1 = bias_part(1, bias_grad(5), (xt_ref[2, 0], xt_ref[2, 1]))
    dxm = dxm_t.T
    tiny_ref[1, 0:1] += col_sum(dxm * nm_ref[...])
    tiny_ref[1, 1:2] += col_sum(dxm)
    tiny_ref[1, 2:2 + HEADS] = dbw1
    send_near(1)
    mg_ref[...] = up_ref[...] + normalise_back(dxm * gain_ref[1:2], nm_ref[...], rm_ref[...])
    arrived(6)
    for row in range(R * R):
        mg_ref[row * D:(row + 1) * D] += get_recv(6, row)

    def bias_grad_0():
        for h in range(HEADS):
            turned = db_ref[0, h].T
            for i in range(R):
                put_stage(5, i * HEADS + h, turned[i * D:(i + 1) * D])
        send_all(7, 5)

    du0_split = backward(0, mg_ref[...], bias_grad_0)
    big_grads(0, (xt_ref[0, 0], xt_ref[0, 1]), du0_split)
    send_big(0)
    send_far(1)
    tiny_ref[0, 6:7] = gate_grad(0)
    tiny_ref[0, 7:8] = col_sum(mg_ref[...])
    dxt_ref[...] = dx_local(0)
    arrived(4)
    for i in range(R):
        for j in range(R):
            row = i * R + j
            new_ref[pl.ds(i * N + j, D, stride=R)] = z_ref[1, row * D:(row + 1) * D] + get_recv(4, row)
    arrived(7)
    dx0_t, dbw0 = bias_part(0, bias_grad(7), (xt_ref[0, 0], xt_ref[0, 1]))
    dx0 = (dxt_ref[...] + dx0_t).T
    tiny_ref[0, 0:1] = col_sum(dx0 * n_ref[0])
    tiny_ref[0, 1:2] = col_sum(dx0)
    tiny_ref[0, 2:2 + HEADS] = dbw0
    send_near(0)
    send_last(1)
    dz0 = normalise_back(dx0 * gain_ref[0:1], n_ref[0], r_ref[0])
    for i in range(R):
        for j in range(R):
            at = (i * R + j) * D
            igrad_ref[pl.ds(i * N + j, D, stride=R)] = mg_ref[at:at + D] + dz0[at:at + D]
    send_far(0)
    finish_big(1)
    send_last(0)
    finish_big(0)

    for k in range(8):
        wait_bytes(recv_ref.at[k, pl.ds(0, D - 1)], send_sem.at[k])
    for b in range(2):
        wait_bytes(bigr_ref.at[b, pl.ds(0, NC - 1)], wsend_sem.at[4 * b])
        wait_bytes(near_ref.at[b, pl.ds(0, near_len - 1)], wsend_sem.at[4 * b + 1])
        if far_len > 1:
            wait_bytes(far_ref.at[b, pl.ds(0, far_len - 1)], wsend_sem.at[4 * b + 2])
        wait_bytes(last_ref.at[b, pl.ds(0, NC - 1)], wsend_sem.at[4 * b + 3])


def body(D, NC, pair, pair_grad, gain, shift, w, bw, gs, wo, os):
    R, N, C = pair.shape[1:]
    T = R * N
    Y = D // Z
    rows = 5 * C // NC
    vmem = pl.BlockSpec(memory_space=pltpu.VMEM)
    out = lambda *shape: jax.ShapeDtypeStruct(shape, F32)
    results = pl.pallas_call(
        functools.partial(kernel, D, NC),
        out_shape=[out(T, C), out(T, C), out(2, C), out(2, C), out(2, 4, C, C), out(2, HEADS, C), out(2, C),
                   out(2, C, C), out(2, C)],
        in_specs=[vmem] * 9,
        out_specs=[vmem] * 9,
        scratch_shapes=[
            pltpu.VMEM((2, T, C), F32),
            pltpu.VMEM((2, T, C), F32),
            pltpu.VMEM((2, T, 1), F32),
            pltpu.VMEM((T, C), F32),
            pltpu.VMEM((T, 1), F32),
            pltpu.VMEM((T, C), F32),
            pltpu.VMEM((T, C), F32),
            pltpu.VMEM((C, T), F32),
            pltpu.VMEM((2, 2, 4 * C, C), BF16),
            pltpu.VMEM((3, 2, C, T), BF16),
            pltpu.VMEM((2, R, 4 * C, N), F32),
            pltpu.VMEM((2, R, HEADS, N, N), F32),
            pltpu.VMEM((2, R, C, N), F32),
            pltpu.VMEM((2, R, C, N), F32),
            pltpu.VMEM((R, C, N), F32),
            pltpu.VMEM((2, R, 4 * C, N), F32),
            pltpu.VMEM((2, HEADS, N, N), F32),
            pltpu.VMEM((2, HEADS, N, N), F32),
            pltpu.VMEM((6, D, R * R, C), F32),
            pltpu.VMEM((2, R * R, N), F32),
            pltpu.VMEM((8, D, R * R, C), F32),
            pltpu.VMEM((2, NC, rows, C), F32),
            pltpu.VMEM((2, NC, rows, C), F32),
            pltpu.VMEM((2, 3, rows + 8, C), F32),
            pltpu.VMEM((2, 4 * Y, rows + 8, C), F32),
            pltpu.VMEM((2, Z // 4, rows + 8, C), F32),
            pltpu.VMEM((2, NC, rows + 8, C), F32),
            pltpu.VMEM((2, 8, C), F32),
            pltpu.SemaphoreType.DMA((8,)),
            pltpu.SemaphoreType.DMA((8,)),
            pltpu.SemaphoreType.DMA((8,)),
            pltpu.SemaphoreType.DMA((8,)),
        ],
        compiler_params=pltpu.CompilerParams(
            collective_id=0, has_side_effects=True, vmem_limit_bytes=56 * 1024 * 1024),
    )(pair.reshape(T, C), pair_grad.reshape(T, C), gain, shift, w, bw, gs, wo, os)
    return (results[0].reshape(pair.shape), results[1].reshape(pair.shape)) + tuple(results[2:])


def solution(mesh):
    rows = P("crop", "dap", None, None)
    return jax.shard_map(
        functools.partial(body, mesh.shape["dap"], mesh.shape["crop"]),
        mesh=mesh,
        in_specs=(rows, rows) + (P(),) * 7,
        out_specs=(rows, rows) + (P(),) * 7,
        check_vma=False,
    )
```

time: 1350 us -> 163 us (0.12)
  waiting for transfers between devices: 966 us -> 0 us
  blocking collectives: 257 us -> 0 us
  Pallas kernels: 0 us -> 155 us
  matrix products: 49.2 us -> 0 us
  local copies, waits for them, and re-layouts: 26.3 us -> 6.94 us
  starting transfers between devices: 18.8 us -> 0 us
  between operations: 14.6 us -> 0.68 us
    psum x3 -> x0, waiting for transfers between devices: 924 us -> none  [the longest x2 568 us: block_backward(): summed = lax.psum(d_bias_full, 'dap')]
    pallas_call x0 -> x1, Pallas kernels: none -> 155 us  [body(): pl.pallas_call(functools.partial(kernel, D, NC), out_shape=[out(T, C), ou...]
    all_gather x2 -> x0, blocking collectives: 135 us -> none  [block_forward(): bias_full = lax.all_gather(bias_rows, 'dap', axis=1, tiled=True)]
    psum x1 -> x0, blocking collectives: 122 us -> none  [body(): totals = lax.psum(stacked_grads, ('crop', 'dap'))]
    dot_general x30 -> x0, matrix products: 49.2 us -> none  [the longest x6 12.3 us: project(): stacked = jnp.einsum('ijc,gcd->gijd', normed, weights, precision=HIGHEST)]
    all_to_all x4 -> x0, waiting for transfers between devices: 42 us -> none  [the longest x1 17.6 us: body(): lax.all_to_all(middle_rows, 'dap', split_axis=1, concat_axis=0, tiled=True)]
    all_to_all x4 -> x0, starting transfers between devices: 18.5 us -> none  [the longest x1 5.86 us: body(): lax.all_to_all(jnp.swapaxes(delta_cols, 0, 1), 'dap', split_axis=0, conca...]
  transfers between devices with their start and end apart: 7 -> 0, of which waited for: 6 -> 0; matrix products, arithmetic and copies ran while one was open for 2% -> 0% of each run, Pallas kernels for 0% -> 0%
where the time goes in v1:
time: 163 us
  Pallas kernels  155 us (95%)
  local copies, waits for them, and re-layouts  6.94 us (4%)
    pallas_call x1, Pallas kernels, body(): pl.pallas_call(functools.partial(kernel, D, NC), out_shape=[out(T, C), ou...  155 us
    unnamed x25, local copies, waits for them, and re-layouts  6.94 us

profile of v1, /device:TPU:1, one launch (start us, length us, event | category | flops | bytes accessed | tf_op | source)
XLA Modules:
  0.0 162.6 jit_solution(8395977379798291384)
XLA Ops:
  0.6 155.0 %shard_map.160 = (f32[512,128]{1,0:T(8,128)}, f32[512,128]{1,0:T(8,128)}, f32[2,128]{1,0:T(2,128)}, f32[2,128]{1,0:T(2,128)}, f32[2,4,128,128]{3,2,1,0:T(8,128)}...) custom-call(f32[512,128]{1,0:T(8,128)} %bitcast.6, f32[512,128]{1,0:T(8,128)} %bitcast.7, ...), custom_call_target="tpu_custom_call" | custom-call | tf_op jit(solution)/shard_map/pallas_call | solution.py:482
  155.6 0.0 copy-start.1
  155.6 0.0 copy-start
  155.7 1.7 %copy.27 = f32[1,4,128,128]{3,2,1,0:T(8,128)} copy(f32[1,4,128,128]{3,2,1,0:T(8,128)} %bitcast.5) | data formatting | bytes 524288
  157.4 0.0 copy-done.1
  157.4 0.0 copy-start.7
  157.4 0.7 copy.28
  158.1 0.0 copy-done.7
  158.1 0.0 copy-start.6
  158.1 0.6 copy.29
  158.7 0.1 copy-done.6
  158.8 0.6 copy.30
  159.3 0.0 copy-done
  159.3 0.0 copy-start.3
  159.3 0.0 copy-start.2
  159.3 0.8 copy.31
  160.1 0.0 copy-done.3
  160.1 0.0 copy-start.5
  160.1 0.6 copy.32
  160.7 0.1 copy-done.5
  160.8 0.6 copy.33
  161.4 0.0 copy-done.2
  161.4 0.0 copy-start.4
  161.4 0.7 copy.34
  162.0 0.0 copy-done.4
  162.0 0.6 copy.35
Async XLA Ops:
  155.6 1.8 %copy-start.1 = (f32[512,128]{1,0:T(8,128)S(1)}, f32[512,128]{1,0:T(8,128)}, u32[]{:S(2)}) copy-start(f32[512,128]{1,0:T(8,128)} %get-tuple-element.19) | copy-start | bytes 786436
  155.6 3.7 %copy-start = (f32[2,4,128,128]{3,2,1,0:T(8,128)S(1)}, f32[2,4,128,128]{3,2,1,0:T(8,128)}, u32[]{:S(2)}) copy-start(f32[2,4,128,128]{3,2,1,0:T(8,128)} %get-tuple-element.40) | copy-start | bytes 1572868
  157.4 0.7 copy-start.7
  158.1 0.7 copy-start.6
  159.3 0.8 copy-start.3
  159.3 2.0 %copy-start.2 = (f32[2,128,128]{2,1,0:T(8,128)S(1)}, f32[2,128,128]{2,1,0:T(8,128)}, u32[]{:S(2)}) copy-start(f32[2,128,128]{2,1,0:T(8,128)} %get-tuple-element.43) | copy-start | bytes 393220
  160.1 0.7 copy-start.5
  161.4 0.7 copy-start.4

commit v2 on v1

v2 whole, which is shorter than its diff:
```python
import functools

import jax
import jax.numpy as jnp
from jax import lax
from jax.experimental import pallas as pl
from jax.experimental.pallas import tpu as pltpu
from jax.sharding import PartitionSpec as P

HEADS = 4
EPSILON = 1e-05
F32 = jnp.float32
BF16 = jnp.bfloat16
MESH = pl.DeviceIdType.MESH
NN = (((1,), (0,)), ((), ()))
NT = (((1,), (1,)), ((), ()))
Z = 16


def split(x):
    hi = x.astype(BF16)
    return hi, (x - hi.astype(F32)).astype(BF16)


def dot(a, b, dims):
    return lax.dot_general(a, b, dims, preferred_element_type=F32)


def dot3(a, b, dims):
    return dot(a[0], b[0], dims) + (dot(a[0], b[1], dims) + dot(a[1], b[0], dims))


def dot3m(a, b, dims):
    rows = a[0].shape[0]
    both = dot(jnp.concatenate(a, axis=0), b[0], dims)
    return both[:rows] + (both[rows:] + dot(a[0], b[1], dims))


def dot_tn(a, b):
    ah, al = split(a)
    bh, bl = split(b)
    stacked = jnp.concatenate([ah.astype(F32), ah.astype(F32), al.astype(F32), al.astype(F32)], axis=0)
    return dot(stacked.T.astype(BF16), jnp.concatenate([bh, bl, bh, bl], axis=0), NN)


def normalise(z):
    center = z - jnp.mean(z, axis=-1, keepdims=True)
    spread = jnp.mean(center * center, axis=-1, keepdims=True)
    r = lax.rsqrt(spread + EPSILON)
    return center * r, r


def normalise_back(dn, n, r):
    first = jnp.mean(dn, axis=-1, keepdims=True)
    second = jnp.mean(dn * n, axis=-1, keepdims=True)
    return r * (dn - first - n * second)


def kernel(
    D,
    NC,
    pair_ref, grad_ref, gain_ref, shift_ref, w_ref, bw_ref, gs_ref, wo_ref, os_ref,
    new_ref, igrad_ref, ggain_ref, gshift_ref, gproj_ref, gbias_ref, ggate_ref, gout_ref, gos_ref,
    z_ref, n_ref, r_ref, nm_ref, rm_ref, up_ref, mg_ref, dx_ref, dxt_ref,
    wt_ref, xt_ref, pt_ref, at_ref, ot_ref, yt_ref, dot_ref, dpt_ref, bt_ref, db_ref,
    stage_ref, chunk_ref, recv_ref, gather_ref, pairsum_ref, zstage_ref, zrecv_ref,
    big_ref, bigr_ref, msg0_ref, msg1_ref, near0_ref, near1_ref, far0_ref, far1_ref, last0_ref, last1_ref,
    tiny_ref, tinyz_ref, tinyp_ref,
    send_sem, recv_sem,
):
    R = 4
    N = R * D
    T = R * N
    C = 128
    HS = C // HEADS
    scale = HS ** (-0.5)
    out_scale = 1.0 / (NC * N)
    me = lax.axis_index("dap")
    crop = lax.axis_index("crop")
    y_at, z_at = me // Z, lax.rem(me, Z)
    block, inner = z_at // 4, lax.rem(z_at, 4)
    NP = 2 * NC
    plane_me = crop * 2 + y_at
    rows = 5 * C // NP

    barrier = pltpu.get_barrier_semaphore()

    def plane_device(p):
        return (p // 2, lax.rem(p, 2) * Z + z_at)

    def z_device(z):
        return (crop, y_at * Z + z)

    partner = (crop, (1 - y_at) * Z + z_at)

    @pl.loop(1, D)
    def _(s):
        pl.semaphore_signal(barrier, inc=1, device_id=(crop, lax.rem(me + s, D)), device_id_type=MESH)

    @pl.loop(1, NP)
    def _(s):
        pl.semaphore_signal(barrier, inc=1, device_id=plane_device(lax.rem(plane_me + s, NP)), device_id_type=MESH)

    def copy_to(src, dst, k, device):
        return pltpu.make_async_remote_copy(
            src_ref=src, dst_ref=dst, send_sem=send_sem.at[k], recv_sem=recv_sem.at[k],
            device_id=device, device_id_type=MESH)

    def wait_bytes(ref, sem):
        pltpu.make_async_copy(ref, ref, sem).wait()

    sent = []

    def arrived(k, ref):
        wait_bytes(ref, recv_sem.at[k])
        sent.append((k, ref))

    def send_half(x, m):
        k = 2 * x + m
        part = pl.ds(8 * m, 8)

        def to(y, z):
            peer = lax.rem(y, 2) * Z + lax.rem(z, Z)
            copy_to(stage_ref.at[x, peer, part], recv_ref.at[x, me, part], k, (crop, peer)).start()

        to(y_at, z_at + 8)
        to(y_at + 1, z_at + 8)

        @pl.loop(1, 8)
        def _(s):
            to(y_at, z_at + 8 - s)
            to(y_at, z_at + 8 + s)
            to(y_at + 1, z_at + 8 - s)
            to(y_at + 1, z_at + 8 + s)

        to(y_at + 1, z_at)
        recv_ref[x, me, part] = stage_ref[x, me, part]

    def half_arrived(x, m):
        arrived(2 * x + m, recv_ref.at[x, pl.ds(0, D - 1), pl.ds(8 * m, 8)])

    def gather_z(g):
        def to(z, k):
            copy_to(chunk_ref.at[g], gather_ref.at[g, me], k, z_device(lax.rem(z, Z))).start()

        @pl.loop(0, 7)
        def _(s):
            to(z_at + 5 + s, 9 + 3 * g)

        @pl.loop(0, 8)
        def _(s):
            to(z_at + 12 + s + s // 4, 8 + 3 * g)

        gather_ref[g, me] = chunk_ref[g]

    def forward(g, z):
        slot = y_at * Z + lax.rem(z, Z)
        copy_to(gather_ref.at[g, slot], gather_ref.at[g, slot], 10 + 3 * g, partner).start()

    def forward_near(g):
        forward(g, z_at)
        arrived(8 + 3 * g, gather_ref.at[g, pl.ds(0, 8)])

        @pl.loop(0, 8)
        def _(s):
            forward(g, z_at + 12 + s + s // 4)

    def forward_far(g):
        arrived(9 + 3 * g, gather_ref.at[g, pl.ds(0, 7)])

        @pl.loop(0, 7)
        def _(s):
            forward(g, z_at + 5 + s)

    def gathered(g):
        arrived(10 + 3 * g, gather_ref.at[g, pl.ds(0, Z)])

    def reduce_y(g):
        copy_to(stage_ref.at[4 + g, pl.ds((1 - y_at) * Z, Z)], pairsum_ref.at[g], 14 + 2 * g, partner).start()

    def reduce_z(g):
        arrived(14 + 2 * g, pairsum_ref.at[g])
        zstage_ref[g] = stage_ref[4 + g, pl.ds(y_at * Z, Z)] + pairsum_ref[g]

        @pl.loop(1, Z)
        def _(s):
            z = lax.rem(z_at + s, Z)
            copy_to(zstage_ref.at[g, z], zrecv_ref.at[g, z_at], 15 + 2 * g, z_device(z)).start()

        zrecv_ref[g, z_at] = zstage_ref[g, z_at]

    def reduced(g):
        arrived(15 + 2 * g, zrecv_ref.at[g, pl.ds(0, Z - 1)])
        total = zrecv_ref[g, 0]
        for p in range(1, Z):
            total = total + zrecv_ref[g, p]
        whole = jnp.concatenate([total[i * HEADS:(i + 1) * HEADS] for i in range(R)], axis=1)
        return jnp.concatenate([whole, jnp.zeros((4, T), F32)], axis=0)

    def put_stage(slot, row, tile):
        stage_ref[slot, :, row, :] = tile

    def get_recv(x, row):
        return recv_ref[x, :, row, :]

    for i in range(R):
        for j in range(R):
            at = (i * R + j) * D
            z_ref[0, at:at + D] = pair_ref[pl.ds(i * N + j, D, stride=R)]
            tile = grad_ref[pl.ds(i * N + j, D, stride=R)]
            up_ref[at:at + D] = tile
            put_stage(0, i * R + j, tile)

    def prepare(b):
        for g in range(4):
            w = w_ref[b, g]
            if g == 0:
                w = w * scale
            hi, lo = split(w.T)
            wt_ref[b, 0, g * C:(g + 1) * C] = hi
            wt_ref[b, 1, g * C:(g + 1) * C] = lo

    def columns(b):
        rows = jnp.concatenate([gs_ref[b:b + 1], jnp.zeros((7, C), F32)], axis=0)
        return rows.T[:, 0:1]

    def bias_rows(b, x_split):
        bw = jnp.concatenate([bw_ref[b], jnp.zeros((4, C), F32)], axis=0)
        return dot3m(split(bw), x_split, NN)

    def put_chunk(slot, rows):
        for i in range(R):
            chunk_ref[slot, i * HEADS:(i + 1) * HEADS] = rows[0:HEADS, i * N:(i + 1) * N]

    def project(b, x_split):
        out = dot3((wt_ref[b, 0], wt_ref[b, 1]), x_split, NN)
        out_gate = jax.nn.sigmoid(out[3 * C:] + columns(b))
        for i in range(R):
            pt_ref[b, i, 0:3 * C] = out[0:3 * C, i * N:(i + 1) * N]
            pt_ref[b, i, 3 * C:] = out_gate[:, i * N:(i + 1) * N]

    def attend(b, lo, hi):
        @pl.loop(lo, hi)
        def _(i):
            for h in range(HEADS):
                at = h * HS
                q = pt_ref[b, i, at:at + HS]
                k = pt_ref[b, i, C + at:C + at + HS]
                v = pt_ref[b, i, 2 * C + at:2 * C + at + HS]
                s = dot_tn(k, q) + bt_ref[b, h]
                e = jnp.exp(s - jnp.max(s, axis=0, keepdims=True))
                a = e * (1.0 / jnp.sum(e, axis=0, keepdims=True))
                at_ref[b, i, h] = a
                o = dot3m(split(v), split(a), NN)
                ot_ref[b, i, at:at + HS] = o
                yt_ref[b, i, at:at + HS] = o * pt_ref[b, i, 3 * C + at:3 * C + at + HS]

    def over_rows(ref, b, lo=0, hi=R):
        return jnp.concatenate([ref[b, i] for i in range(lo, hi)], axis=1)

    def update(b, lo, hi):
        ut = dot3(split(wo_ref[b].T), split(over_rows(yt_ref, b, lo, hi)), NN)
        return ut.T + os_ref[b:b + 1]

    def backward(b, du, put_bias_grad):
        du_split = split(du)
        dyt = dot3(split(wo_ref[b]), du_split, NT)
        for i in range(R):
            dy = dyt[:, i * N:(i + 1) * N]
            gate = pt_ref[b, i, 3 * C:]
            dot_ref[i] = dy * gate
            dpt_ref[b, i, 3 * C:] = dy * ot_ref[b, i] * (gate * (1.0 - gate))
        db_ref[b] = jnp.zeros((HEADS, N, N), F32)

        @pl.loop(0, R)
        def _(i):
            for h in range(HEADS):
                at = h * HS
                q = pt_ref[b, i, at:at + HS]
                k = pt_ref[b, i, C + at:C + at + HS]
                v = pt_ref[b, i, 2 * C + at:2 * C + at + HS]
                a = at_ref[b, i, h]
                do = dot_ref[i, at:at + HS]
                row = jnp.sum(do * ot_ref[b, i, at:at + HS], axis=0, keepdims=True)
                ds = a * (dot_tn(v, do) - row)
                db_ref[b, h] += ds
                ds_split = split(ds)
                dpt_ref[b, i, at:at + HS] = dot3m(split(k), ds_split, NN)
                dpt_ref[b, i, C + at:C + at + HS] = dot3m(split(q), ds_split, NT)
                dpt_ref[b, i, 2 * C + at:2 * C + at + HS] = dot3m(split(do), split(a), NT)
        put_bias_grad()
        return du_split

    def dx_local(b, lo, hi):
        total = None
        for g in range(4):
            w = w_ref[b, g]
            if g == 0:
                w = w * scale
            d = jnp.concatenate([dpt_ref[b, i, g * C:(g + 1) * C] for i in range(lo, hi)], axis=1)
            term = dot3(split(w), split(d), NN)
            total = term if total is None else total + term
        return total

    msgs, nears, fars, lasts = (msg0_ref, msg1_ref), (near0_ref, near1_ref), (far0_ref, far1_ref), (last0_ref, last1_ref)

    def big_grads(b, x_split, du_split):
        parts = []
        for g in range(4):
            d = jnp.concatenate([dpt_ref[b, i, g * C:(g + 1) * C] for i in range(R)], axis=1)
            out = dot3(x_split, split(d), NT)
            parts.append(out * scale if g == 0 else out)
        parts.append(dot3(split(over_rows(yt_ref, b)), du_split, NN))
        whole = jnp.concatenate(parts, axis=0)
        for p in range(NP):
            big_ref[b, p] = whole[p * rows:(p + 1) * rows]

    def to_plane(src_of, dst, k):
        @pl.loop(1, NP)
        def _(s):
            p = lax.rem(plane_me + s, NP)
            copy_to(src_of(p), dst, k, plane_device(p)).start()

    def send_big(b):
        to_plane(lambda p: big_ref.at[b, p], bigr_ref.at[b, plane_me], 18 + 4 * b)
        bigr_ref[b, plane_me] = big_ref[b, plane_me]

    def total_of(ref, count):
        total = ref[0]
        for p in range(1, count):
            total = total + ref[p]
        return total

    def send_near(b):
        arrived(18 + 4 * b, bigr_ref.at[b, pl.ds(0, NP - 1)])
        msgs[b][0, 0:rows] = total_of(bigr_ref.at[b], NP)
        if b == 1:
            msgs[b][0, rows:rows + 8] = tiny_ref[b]

        @pl.loop(1, 4)
        def _(s):
            m = lax.rem(inner + s, 4)
            copy_to(msgs[b].at[0], nears[b].at[inner], 19 + 4 * b, z_device(block * 4 + m)).start()

        nears[b][inner] = msgs[b][0]

    def send_far(b):
        arrived(19 + 4 * b, nears[b].at[pl.ds(0, 3)])
        msgs[b][1] = total_of(nears[b], 4)

        @pl.loop(1, 4)
        def _(s):
            m = lax.rem(block + s, 4)
            copy_to(msgs[b].at[1], fars[b].at[block], 20 + 4 * b, z_device(m * 4 + inner)).start()

        fars[b][block] = msgs[b][1]

    def send_last(b):
        arrived(20 + 4 * b, fars[b].at[pl.ds(0, 3)])
        msgs[b][2] = total_of(fars[b], 4) * out_scale
        to_plane(lambda p: msgs[b].at[2], lasts[b].at[plane_me], 21 + 4 * b)
        lasts[b][plane_me] = msgs[b][2]

    def finish_big(b):
        arrived(21 + 4 * b, lasts[b].at[pl.ds(0, NP - 1)])
        for p in range(NP):
            first = p * rows
            while first < (p + 1) * rows:
                g, at = first // C, first % C
                count = min((p + 1) * rows - first, C - at)
                piece = lasts[b][p, first - p * rows:first - p * rows + count]
                if g < 4:
                    gproj_ref[b, g, at:at + count] = piece
                else:
                    gout_ref[b, at:at + count] = piece
                first += count

    def put_tiny(b, tiny):
        ggain_ref[b:b + 1] = tiny[0:1]
        gshift_ref[b:b + 1] = tiny[1:2]
        gbias_ref[b] = tiny[2:2 + HEADS]
        ggate_ref[b:b + 1] = tiny[6:7]
        gos_ref[b:b + 1] = tiny[7:8]

    def send_tiny_z():
        @pl.loop(1, Z)
        def _(s):
            copy_to(tiny_ref.at[0], tinyz_ref.at[z_at], 26, z_device(lax.rem(z_at + s, Z))).start()

        tinyz_ref[z_at] = tiny_ref[0]

    def send_tiny_plane():
        arrived(26, tinyz_ref.at[pl.ds(0, Z - 1)])
        tiny_ref[2] = total_of(tinyz_ref, Z)
        to_plane(lambda p: tiny_ref.at[2], tinyp_ref.at[plane_me], 27)
        tinyp_ref[plane_me] = tiny_ref[2]

    def finish_tiny():
        arrived(27, tinyp_ref.at[pl.ds(0, NP - 1)])
        put_tiny(0, total_of(tinyp_ref, NP) * out_scale)

    def gate_grad(b):
        total = None
        for i in range(R):
            d = dpt_ref[b, i, 3 * C:]
            total = d if total is None else total + d
        return jnp.sum(total.T, axis=0, keepdims=True)

    def bias_part(b, dbr, x_split):
        bw = jnp.concatenate([bw_ref[b], jnp.zeros((4, C), F32)], axis=0)
        d_split = split(dbr)
        dxt = dot3(split(bw.T), d_split, NN)
        dbw = dot3m(d_split, x_split, NT)
        return dxt, dbw[0:HEADS]

    def col_sum(x):
        return jnp.sum(x, axis=0, keepdims=True)

    n0, r0 = normalise(z_ref[0])
    n_ref[0] = n0
    r_ref[0] = r0
    x0_split = split((n0 * gain_ref[0:1] + shift_ref[0:1]).T)
    xt_ref[0, 0] = x0_split[0]
    xt_ref[0, 1] = x0_split[1]
    put_chunk(0, bias_rows(0, x0_split))
    pl.semaphore_wait(barrier, D - 1 + NP - 1)
    gather_z(0)
    prepare(0)
    forward_near(0)
    project(0, x0_split)
    forward_far(0)
    send_half(0, 0)
    prepare(1)
    gathered(0)
    for h in range(HEADS):
        bt_ref[0, h] = jnp.concatenate([gather_ref[0, :, i * HEADS + h, :] for i in range(R)], axis=0).T

    for m in range(2):
        attend(0, 2 * m, 2 * m + 2)
        part = slice(2 * m * N, (2 * m + 2) * N)
        z_ref[1, part] = z_ref[0, part] + update(0, 2 * m, 2 * m + 2)
        for row in range(8 * m, 8 * m + 8):
            put_stage(1, row, z_ref[1, row * D:(row + 1) * D])
        if m == 0:
            send_half(1, 0)
    nm, rm = normalise(z_ref[1])
    nm_ref[...] = nm
    rm_ref[...] = rm
    xm_split = split((nm * gain_ref[1:2] + shift_ref[1:2]).T)
    xt_ref[2, 0] = xm_split[0]
    xt_ref[2, 1] = xm_split[1]
    put_chunk(1, bias_rows(1, xm_split))
    gather_z(1)
    send_half(1, 1)
    forward_near(1)
    forward_far(1)
    send_half(0, 1)

    half_arrived(1, 0)
    half_arrived(1, 1)

    def columns_layout(x):
        return jnp.concatenate([get_recv(x, i * R + j) for j in range(R) for i in range(R)], axis=0)

    n1, r1 = normalise(columns_layout(1))
    n_ref[1] = n1
    r_ref[1] = r1
    x1_split = split((n1 * gain_ref[1:2] + shift_ref[1:2]).T)
    xt_ref[1, 0] = x1_split[0]
    xt_ref[1, 1] = x1_split[1]
    project(1, x1_split)
    gathered(1)
    for h in range(HEADS):
        bt_ref[1, h] = jnp.concatenate([gather_ref[1, :, i * HEADS + h, :] for i in range(R)], axis=0)

    def stage_back(slot, m, value):
        for row in range(8):
            put_stage(slot, 8 * m + row, value[row * D:(row + 1) * D])

    attend(1, 0, R)
    u1 = update(1, 0, R)
    stage_back(2, 0, u1[0:2 * N])
    stage_back(2, 1, u1[2 * N:])
    send_half(2, 0)

    half_arrived(0, 0)
    half_arrived(0, 1)
    du1 = columns_layout(0)

    def bias_grad_1():
        for h in range(HEADS):
            for i in range(R):
                put_stage(4, i * HEADS + h, db_ref[1, h, i * D:(i + 1) * D])
        reduce_y(0)

    du1_split = backward(1, du1, bias_grad_1)
    for m in range(2):
        part = slice(2 * m * N, (2 * m + 2) * N)
        dx = dx_local(1, 2 * m, 2 * m + 2).T
        dx_ref[part] = dx
        stage_back(3, m, normalise_back(dx * gain_ref[1:2], n_ref[1, part], r_ref[1, part]))
        send_half(3, m)
    reduce_z(0)
    big_grads(1, (xt_ref[1, 0], xt_ref[1, 1]), du1_split)
    send_big(1)
    tiny_ref[1, 0:1] = col_sum(dx_ref[...] * n_ref[1])
    tiny_ref[1, 1:2] = col_sum(dx_ref[...])
    tiny_ref[1, 6:7] = gate_grad(1)
    tiny_ref[1, 7:8] = col_sum(du1)
    dxm_t, dbw1 = bias_part(1, reduced(0), (xt_ref[2, 0], xt_ref[2, 1]))
    dxm = dxm_t.T
    tiny_ref[1, 0:1] += col_sum(dxm * nm_ref[...])
    tiny_ref[1, 1:2] += col_sum(dxm)
    tiny_ref[1, 2:2 + HEADS] = dbw1
    mg_ref[...] = up_ref[...] + normalise_back(dxm * gain_ref[1:2], nm_ref[...], rm_ref[...])
    send_near(1)
    half_arrived(3, 0)
    half_arrived(3, 1)
    send_half(2, 1)
    for i in range(R):
        for j in range(R):
            at = (i * R + j) * D
            mg_ref[at:at + D] += get_recv(3, j * R + i)

    def bias_grad_0():
        for h in range(HEADS):
            turned = db_ref[0, h].T
            for i in range(R):
                put_stage(5, i * HEADS + h, turned[i * D:(i + 1) * D])
        reduce_y(1)

    du0_split = backward(0, mg_ref[...], bias_grad_0)
    send_far(1)
    big_grads(0, (xt_ref[0, 0], xt_ref[0, 1]), du0_split)
    reduce_z(1)
    send_big(0)
    tiny_ref[0, 6:7] = gate_grad(0)
    tiny_ref[0, 7:8] = col_sum(mg_ref[...])
    dxt_ref[...] = dx_local(0, 0, R)
    half_arrived(2, 0)
    half_arrived(2, 1)
    for i in range(R):
        for j in range(R):
            at = (i * R + j) * D
            new_ref[pl.ds(i * N + j, D, stride=R)] = z_ref[1, at:at + D] + get_recv(2, j * R + i)
    send_last(1)
    send_near(0)
    dx0_t, dbw0 = bias_part(0, reduced(1), (xt_ref[0, 0], xt_ref[0, 1]))
    dx_ref[...] = (dxt_ref[...] + dx0_t).T
    tiny_ref[0, 0:1] = col_sum(dx_ref[...] * n_ref[0])
    tiny_ref[0, 1:2] = col_sum(dx_ref[...])
    tiny_ref[0, 2:2 + HEADS] = dbw0
    send_tiny_z()
    send_far(0)
    dz0 = normalise_back(dx_ref[...] * gain_ref[0:1], n_ref[0], r_ref[0])
    for i in range(R):
        for j in range(R):
            at = (i * R + j) * D
            igrad_ref[pl.ds(i * N + j, D, stride=R)] = mg_ref[at:at + D] + dz0[at:at + D]
    send_tiny_plane()
    finish_big(1)
    tiny1 = last1_ref[0, rows:rows + 8]
    for p in range(1, NP):
        tiny1 = tiny1 + last1_ref[p, rows:rows + 8]
    put_tiny(1, tiny1)
    send_last(0)
    finish_tiny()
    finish_big(0)

    for k, ref in sent:
        wait_bytes(ref, send_sem.at[k])


def copies(*refs):
    count = len(refs) // 2
    for k in range(count):
        refs[count + k][...] = refs[k][...]


def body(D, NC, pair, pair_grad, gain, shift, w, bw, gs, wo, os):
    R, N, C = pair.shape[1:]
    T = R * N
    NP = 2 * NC
    rows = 5 * C // NP
    vmem = pl.BlockSpec(memory_space=pltpu.VMEM)
    out = lambda *shape: jax.ShapeDtypeStruct(shape, F32)
    results = pl.pallas_call(
        functools.partial(kernel, D, NC),
        out_shape=[out(T, C), out(T, C), out(2, C), out(2, C), out(2, 4, C, C), out(2, HEADS, C), out(2, C),
                   out(2, C, C), out(2, C)],
        in_specs=[vmem] * 9,
        out_specs=[vmem] * 9,
        scratch_shapes=[
            pltpu.VMEM((2, T, C), F32),
            pltpu.VMEM((2, T, C), F32),
            pltpu.VMEM((2, T, 1), F32),
            pltpu.VMEM((T, C), F32),
            pltpu.VMEM((T, 1), F32),
            pltpu.VMEM((T, C), F32),
            pltpu.VMEM((T, C), F32),
            pltpu.VMEM((T, C), F32),
            pltpu.VMEM((C, T), F32),
            pltpu.VMEM((2, 2, 4 * C, C), BF16),
            pltpu.VMEM((3, 2, C, T), BF16),
            pltpu.VMEM((2, R, 4 * C, N), F32),
            pltpu.VMEM((2, R, HEADS, N, N), F32),
            pltpu.VMEM((2, R, C, N), F32),
            pltpu.VMEM((2, R, C, N), F32),
            pltpu.VMEM((R, C, N), F32),
            pltpu.VMEM((2, R, 4 * C, N), F32),
            pltpu.VMEM((2, HEADS, N, N), F32),
            pltpu.VMEM((2, HEADS, N, N), F32),
            pltpu.VMEM((6, D, R * R, C), F32),
            pltpu.VMEM((2, R * R, N), F32),
            pltpu.VMEM((4, D, R * R, C), F32),
            pltpu.VMEM((2, D, R * R, C), F32),
            pltpu.VMEM((2, Z, R * R, C), F32),
            pltpu.VMEM((2, Z, R * R, C), F32),
            pltpu.VMEM((2, Z, R * R, C), F32),
            pltpu.VMEM((2, NP, rows, C), F32),
            pltpu.VMEM((2, NP, rows, C), F32),
            pltpu.VMEM((3, rows, C), F32),
            pltpu.VMEM((3, rows + 8, C), F32),
            pltpu.VMEM((4, rows, C), F32),
            pltpu.VMEM((4, rows + 8, C), F32),
            pltpu.VMEM((4, rows, C), F32),
            pltpu.VMEM((4, rows + 8, C), F32),
            pltpu.VMEM((NP, rows, C), F32),
            pltpu.VMEM((NP, rows + 8, C), F32),
            pltpu.VMEM((3, 8, C), F32),
            pltpu.VMEM((Z, 8, C), F32),
            pltpu.VMEM((NP, 8, C), F32),
            pltpu.SemaphoreType.DMA((28,)),
            pltpu.SemaphoreType.DMA((28,)),
        ],
        compiler_params=pltpu.CompilerParams(
            collective_id=0, has_side_effects=True, vmem_limit_bytes=56 * 1024 * 1024),
    )(pair.reshape(T, C), pair_grad.reshape(T, C), gain, shift, w, bw, gs, wo, os)
    results = pl.pallas_call(
        copies,
        out_shape=[jax.ShapeDtypeStruct(r.shape, F32) for r in results],
        in_specs=[vmem] * 9,
        out_specs=[vmem] * 9,
        compiler_params=pltpu.CompilerParams(vmem_limit_bytes=16 * 1024 * 1024),
    )(*results)
    return (results[0].reshape(pair.shape), results[1].reshape(pair.shape)) + tuple(results[2:])


def solution(mesh):
    rows = P("crop", "dap", None, None)
    return jax.shard_map(
        functools.partial(body, mesh.shape["dap"], mesh.shape["crop"]),
        mesh=mesh,
        in_specs=(rows, rows) + (P(),) * 7,
        out_specs=(rows, rows) + (P(),) * 7,
        check_vma=False,
    )
```

time: 163 us -> 133 us (0.82)
  Pallas kernels: 155 us -> 127 us
  local copies, waits for them, and re-layouts: 6.94 us -> 4.52 us
    pallas_call x1, Pallas kernels: 155 us -> 126 us  [body(): pl.pallas_call(functools.partial(kernel, D, NC), out_shape=[out(T, C), ou...]
    unnamed x25 -> x18, local copies, waits for them, and re-layouts: 6.94 us -> 4.52 us
where the time goes in v2:
time: 133 us; the launch traced here: 132 us
  Pallas kernels  127 us (95%)
  local copies, waits for them, and re-layouts  4.52 us (3%)
    pallas_call x1, Pallas kernels, body(): pl.pallas_call(functools.partial(kernel, D, NC), out_shape=[out(T, C), ou...  126 us
    unnamed x18, local copies, waits for them, and re-layouts  4.52 us

profile of v2, /device:TPU:1, one launch (start us, length us, event | category | flops | bytes accessed | tf_op | source)
XLA Modules:
  0.0 132.5 jit_solution(2329024562139361770)
XLA Ops:
  0.6 126.2 %shard_map.160 = (f32[512,128]{1,0:T(8,128)}, f32[512,128]{1,0:T(8,128)}, f32[2,128]{1,0:T(2,128)}, f32[2,128]{1,0:T(2,128)}, f32[2,4,128,128]{3,2,1,0:T(8,128)}...) custom-call(f32[512,128]{1,0:T(8,128)} %bitcast.4, f32[512,128]{1,0:T(8,128)} %bitcast.5, ...), custom_call_target="tpu_custom_call" | custom-call | tf_op jit(solution)/shard_map/pallas_call | solution.py:587
  126.8 0.0 copy-start.8
  126.8 0.0 copy-start.4
  126.8 0.0 copy-start.6
  126.9 0.0 copy-start.7
  126.9 0.0 copy-start.5
  126.9 0.6 copy-done.8
  127.5 0.0 copy-done.4
  127.5 0.0 copy-done.6
  127.5 0.0 copy-done.7
  127.5 0.0 copy-done.5
  127.5 0.0 copy-start
  127.5 1.0 copy-done
  128.6 0.0 copy-start.1
  128.6 0.9 copy-done.1
  129.5 0.0 copy-start.2
  129.5 0.9 copy-done.2
  130.5 0.0 copy-start.3
  130.5 0.9 copy-done.3
  131.4 1.1 shard_map.161
Async XLA Ops:
  126.8 0.7 copy-start.8
  126.8 0.7 copy-start.4
  126.8 0.7 copy-start.6
  126.9 0.7 copy-start.7
  126.9 0.7 copy-start.5
  127.5 1.0 copy-start
  128.6 0.9 copy-start.1
  129.5 0.9 copy-start.2
  130.5 0.9 copy-start.3

commit v3 on v2

--- a/solution.py
+++ b/solution.py
@@ -59,15 +59,26 @@
 def kernel(
     D,
     NC,
-    pair_ref, grad_ref, gain_ref, shift_ref, w_ref, bw_ref, gs_ref, wo_ref, os_ref,
-    new_ref, igrad_ref, ggain_ref, gshift_ref, gproj_ref, gbias_ref, ggate_ref, gout_ref, gos_ref,
+    *refs,
+):
+    given, results, held, filled, refs = refs[:9], refs[9:18], refs[18:27], refs[27:36], refs[36:]
+    body_of(D, NC, given, results, held, filled, *refs)
+
+
+def body_of(
+    D,
+    NC,
+    given, results, held, filled,
+    in_sem, out_sem,
     z_ref, n_ref, r_ref, nm_ref, rm_ref, up_ref, mg_ref, dx_ref, dxt_ref,
     wt_ref, xt_ref, pt_ref, at_ref, ot_ref, yt_ref, dot_ref, dpt_ref, bt_ref, db_ref,
-    stage_ref, chunk_ref, recv_ref, gather_ref, pairsum_ref, zstage_ref, zrecv_ref,
+    stage_ref, chunk_ref, recv_ref, gather_ref, pairsum_ref, zstage_ref, zrecv_ref, direct_ref,
     big_ref, bigr_ref, msg0_ref, msg1_ref, near0_ref, near1_ref, far0_ref, far1_ref, last0_ref, last1_ref,
     tiny_ref, tinyz_ref, tinyp_ref,
     send_sem, recv_sem,
 ):
+    pair_ref, grad_ref, gain_ref, shift_ref, w_ref, bw_ref, gs_ref, wo_ref, os_ref = held
+    new_ref, igrad_ref, ggain_ref, gshift_ref, gproj_ref, gbias_ref, ggate_ref, gout_ref, gos_ref = filled
     R = 4
     N = R * D
     T = R * N
@@ -93,13 +104,30 @@
 
     partner = (crop, (1 - y_at) * Z + z_at)
 
-    @pl.loop(1, D)
+    def greet(y, z):
+        device = (crop, lax.rem(y, 2) * Z + lax.rem(z, Z))
+        pl.semaphore_signal(barrier, inc=1, device_id=device, device_id_type=MESH)
+
+    greet(y_at, z_at + 8)
+    greet(y_at + 1, z_at + 8)
+
+    @pl.loop(1, 8)
     def _(s):
-        pl.semaphore_signal(barrier, inc=1, device_id=(crop, lax.rem(me + s, D)), device_id_type=MESH)
+        greet(y_at, z_at + 8 - s)
+        greet(y_at, z_at + 8 + s)
+        greet(y_at + 1, z_at + 8 - s)
+        greet(y_at + 1, z_at + 8 + s)
+
+    greet(y_at + 1, z_at)
 
     @pl.loop(1, NP)
     def _(s):
         pl.semaphore_signal(barrier, inc=1, device_id=plane_device(lax.rem(plane_me + s, NP)), device_id_type=MESH)
+
+    fetches = [pltpu.make_async_copy(given[k], held[k], in_sem.at[k]) for k in range(9)]
+    stores = [pltpu.make_async_copy(filled[k], results[k], out_sem.at[k]) for k in range(9)]
+    for k in (0, 2, 3, 5, 4, 6, 1, 7, 8):
+        fetches[k].start()
 
     def copy_to(src, dst, k, device):
         return pltpu.make_async_remote_copy(
@@ -139,77 +167,125 @@
     def half_arrived(x, m):
         arrived(2 * x + m, recv_ref.at[x, pl.ds(0, D - 1), pl.ds(8 * m, 8)])
 
+    def near_z(s):
+        return lax.rem(z_at + 12 + s + s // 4, Z)
+
+    def middle_z(s):
+        return lax.rem(z_at + 5 + s + 3 * (s // 2), Z)
+
+    def far_z(s):
+        return lax.rem(z_at + 7 + s, Z)
+
     def gather_z(g):
-        def to(z, k):
-            copy_to(chunk_ref.at[g], gather_ref.at[g, me], k, z_device(lax.rem(z, Z))).start()
-
-        @pl.loop(0, 7)
-        def _(s):
-            to(z_at + 5 + s, 9 + 3 * g)
+        def to(y, z, k):
+            copy_to(chunk_ref.at[g], gather_ref.at[g, me], k, (crop, y * Z + z)).start()
+
+        @pl.loop(0, 3)
+        def _(s):
+            to(y_at, far_z(s), 10 + 4 * g)
+            if g == 0:
+                to(1 - y_at, far_z(s), 10 + 4 * g)
+
+        @pl.loop(0, 4)
+        def _(s):
+            to(y_at, middle_z(s), 9 + 4 * g)
 
         @pl.loop(0, 8)
         def _(s):
-            to(z_at + 12 + s + s // 4, 8 + 3 * g)
+            to(y_at, near_z(s), 8 + 4 * g)
 
         gather_ref[g, me] = chunk_ref[g]
 
-    def forward(g, z):
-        slot = y_at * Z + lax.rem(z, Z)
-        copy_to(gather_ref.at[g, slot], gather_ref.at[g, slot], 10 + 3 * g, partner).start()
-
-    def forward_near(g):
-        forward(g, z_at)
-        arrived(8 + 3 * g, gather_ref.at[g, pl.ds(0, 8)])
+    def forward(g):
+        def to(z):
+            slot = y_at * Z + z
+            copy_to(gather_ref.at[g, slot], gather_ref.at[g, slot], 11 + 4 * g, partner).start()
+
+        to(z_at)
+        arrived(8 + 4 * g, gather_ref.at[g, pl.ds(0, 8)])
 
         @pl.loop(0, 8)
         def _(s):
-            forward(g, z_at + 12 + s + s // 4)
-
-    def forward_far(g):
-        arrived(9 + 3 * g, gather_ref.at[g, pl.ds(0, 7)])
-
-        @pl.loop(0, 7)
-        def _(s):
-            forward(g, z_at + 5 + s)
+            to(near_z(s))
+
+        arrived(9 + 4 * g, gather_ref.at[g, pl.ds(0, 4)])
+
+        @pl.loop(0, 4)
+        def _(s):
+            to(middle_z(s))
+
+        if g == 1:
+            arrived(10 + 4 * g, gather_ref.at[g, pl.ds(0, 3)])
+
+            @pl.loop(0, 3)
+            def _(s):
+                to(far_z(s))
 
     def gathered(g):
-        arrived(10 + 3 * g, gather_ref.at[g, pl.ds(0, Z)])
-
-    def reduce_y(g):
-        copy_to(stage_ref.at[4 + g, pl.ds((1 - y_at) * Z, Z)], pairsum_ref.at[g], 14 + 2 * g, partner).start()
-
-    def reduce_z(g):
-        arrived(14 + 2 * g, pairsum_ref.at[g])
-        zstage_ref[g] = stage_ref[4 + g, pl.ds(y_at * Z, Z)] + pairsum_ref[g]
+        if g == 0:
+            arrived(10, gather_ref.at[g, pl.ds(0, 6)])
+        arrived(11 + 4 * g, gather_ref.at[g, pl.ds(0, 13 + 3 * g)])
+
+    def reduce_y():
+        copy_to(stage_ref.at[4, pl.ds((1 - y_at) * Z, Z)], pairsum_ref.at[0], 16, partner).start()
+
+    def reduce_z():
+        arrived(16, pairsum_ref.at[0])
+        zstage_ref[0] = stage_ref[4, pl.ds(y_at * Z, Z)] + pairsum_ref[0]
 
         @pl.loop(1, Z)
         def _(s):
             z = lax.rem(z_at + s, Z)
-            copy_to(zstage_ref.at[g, z], zrecv_ref.at[g, z_at], 15 + 2 * g, z_device(z)).start()
-
-        zrecv_ref[g, z_at] = zstage_ref[g, z_at]
-
-    def reduced(g):
-        arrived(15 + 2 * g, zrecv_ref.at[g, pl.ds(0, Z - 1)])
-        total = zrecv_ref[g, 0]
-        for p in range(1, Z):
-            total = total + zrecv_ref[g, p]
+            copy_to(zstage_ref.at[0, z], zrecv_ref.at[0, z_at], 17, z_device(z)).start()
+
+        zrecv_ref[0, z_at] = zstage_ref[0, z_at]
+
+    def swift_y():
+        @pl.loop(0, 5)
+        def _(s):
+            z = lax.rem(z_at + 6 + s, Z)
+            copy_to(stage_ref.at[5, y_at * Z + z], direct_ref.at[s], 28, (crop, y_at * Z + z)).start()
+            other = (1 - y_at) * Z + z
+            copy_to(stage_ref.at[5, other], direct_ref.at[5 + s], 28, (crop, other)).start()
+
+        @pl.loop(0, 11)
+        def _(s):
+            z = lax.rem(z_at + 11 + s, Z)
+            copy_to(stage_ref.at[5, (1 - y_at) * Z + z], pairsum_ref.at[1, s], 18, partner).start()
+
+    def swift_z():
+        arrived(18, pairsum_ref.at[1, pl.ds(0, 11)])
+
+        @pl.loop(0, 11)
+        def _(s):
+            z = lax.rem(z_at + 11 + s, Z)
+            zstage_ref[1, s] = stage_ref[5, y_at * Z + z] + pairsum_ref[1, s]
+
+        @pl.loop(0, 5)
+        def _(s):
+            for at in (s, 10 - s):
+                copy_to(zstage_ref.at[1, at], zrecv_ref.at[1, at], 19, z_device(lax.rem(z_at + 11 + at, Z))).start()
+
+        zrecv_ref[1, 5] = zstage_ref[1, 5]
+
+    def token_rows(total):
         whole = jnp.concatenate([total[i * HEADS:(i + 1) * HEADS] for i in range(R)], axis=1)
         return jnp.concatenate([whole, jnp.zeros((4, T), F32)], axis=0)
 
+    def reduced():
+        arrived(17, zrecv_ref.at[0, pl.ds(0, Z - 1)])
+        return token_rows(total_of(zrecv_ref.at[0], Z))
+
+    def swift_reduced():
+        arrived(28, direct_ref)
+        arrived(19, zrecv_ref.at[1, pl.ds(0, 10)])
+        return token_rows(total_of(zrecv_ref.at[1], 11) + total_of(direct_ref, 10))
+
     def put_stage(slot, row, tile):
         stage_ref[slot, :, row, :] = tile
 
     def get_recv(x, row):
         return recv_ref[x, :, row, :]
-
-    for i in range(R):
-        for j in range(R):
-            at = (i * R + j) * D
-            z_ref[0, at:at + D] = pair_ref[pl.ds(i * N + j, D, stride=R)]
-            tile = grad_ref[pl.ds(i * N + j, D, stride=R)]
-            up_ref[at:at + D] = tile
-            put_stage(0, i * R + j, tile)
 
     def prepare(b):
         for g in range(4):
@@ -240,8 +316,7 @@
             pt_ref[b, i, 3 * C:] = out_gate[:, i * N:(i + 1) * N]
 
     def attend(b, lo, hi):
-        @pl.loop(lo, hi)
-        def _(i):
+        for i in range(lo, hi):
             for h in range(HEADS):
                 at = h * HS
                 q = pt_ref[b, i, at:at + HS]
@@ -262,18 +337,14 @@
         ut = dot3(split(wo_ref[b].T), split(over_rows(yt_ref, b, lo, hi)), NN)
         return ut.T + os_ref[b:b + 1]
 
-    def backward(b, du, put_bias_grad):
-        du_split = split(du)
+    def backward(b, du_split, lo, hi):
         dyt = dot3(split(wo_ref[b]), du_split, NT)
-        for i in range(R):
-            dy = dyt[:, i * N:(i + 1) * N]
+        for i in range(lo, hi):
+            dy = dyt[:, (i - lo) * N:(i - lo + 1) * N]
             gate = pt_ref[b, i, 3 * C:]
             dot_ref[i] = dy * gate
             dpt_ref[b, i, 3 * C:] = dy * ot_ref[b, i] * (gate * (1.0 - gate))
-        db_ref[b] = jnp.zeros((HEADS, N, N), F32)
-
-        @pl.loop(0, R)
-        def _(i):
+        for i in range(lo, hi):
             for h in range(HEADS):
                 at = h * HS
                 q = pt_ref[b, i, at:at + HS]
@@ -283,13 +354,14 @@
                 do = dot_ref[i, at:at + HS]
                 row = jnp.sum(do * ot_ref[b, i, at:at + HS], axis=0, keepdims=True)
                 ds = a * (dot_tn(v, do) - row)
-                db_ref[b, h] += ds
+                if i == 0:
+                    db_ref[b, h] = ds
+                else:
+                    db_ref[b, h] += ds
                 ds_split = split(ds)
                 dpt_ref[b, i, at:at + HS] = dot3m(split(k), ds_split, NN)
                 dpt_ref[b, i, C + at:C + at + HS] = dot3m(split(q), ds_split, NT)
                 dpt_ref[b, i, 2 * C + at:2 * C + at + HS] = dot3m(split(do), split(a), NT)
-        put_bias_grad()
-        return du_split
 
     def dx_local(b, lo, hi):
         total = None
@@ -316,13 +388,19 @@
             big_ref[b, p] = whole[p * rows:(p + 1) * rows]
 
     def to_plane(src_of, dst, k):
-        @pl.loop(1, NP)
-        def _(s):
+        def to(s):
             p = lax.rem(plane_me + s, NP)
             copy_to(src_of(p), dst, k, plane_device(p)).start()
 
+        to(NC)
+
+        @pl.loop(1, NC)
+        def _(s):
+            to(NC - s)
+            to(NC + s)
+
     def send_big(b):
-        to_plane(lambda p: big_ref.at[b, p], bigr_ref.at[b, plane_me], 18 + 4 * b)
+        to_plane(lambda p: big_ref.at[b, p], bigr_ref.at[b, plane_me], 20 + 4 * b)
         bigr_ref[b, plane_me] = big_ref[b, plane_me]
 
     def total_of(ref, count):
@@ -332,7 +410,7 @@
         return total
 
     def send_near(b):
-        arrived(18 + 4 * b, bigr_ref.at[b, pl.ds(0, NP - 1)])
+        arrived(20 + 4 * b, bigr_ref.at[b, pl.ds(0, NP - 1)])
         msgs[b][0, 0:rows] = total_of(bigr_ref.at[b], NP)
         if b == 1:
             msgs[b][0, rows:rows + 8] = tiny_ref[b]
@@ -340,29 +418,29 @@
         @pl.loop(1, 4)
         def _(s):
             m = lax.rem(inner + s, 4)
-            copy_to(msgs[b].at[0], nears[b].at[inner], 19 + 4 * b, z_device(block * 4 + m)).start()
+            copy_to(msgs[b].at[0], nears[b].at[inner], 21 + 4 * b, z_device(block * 4 + m)).start()
 
         nears[b][inner] = msgs[b][0]
 
     def send_far(b):
-        arrived(19 + 4 * b, nears[b].at[pl.ds(0, 3)])
+        arrived(21 + 4 * b, nears[b].at[pl.ds(0, 3)])
         msgs[b][1] = total_of(nears[b], 4)
 
         @pl.loop(1, 4)
         def _(s):
             m = lax.rem(block + s, 4)
-            copy_to(msgs[b].at[1], fars[b].at[block], 20 + 4 * b, z_device(m * 4 + inner)).start()
+            copy_to(msgs[b].at[1], fars[b].at[block], 22 + 4 * b, z_device(m * 4 + inner)).start()
 
         fars[b][block] = msgs[b][1]
 
     def send_last(b):
-        arrived(20 + 4 * b, fars[b].at[pl.ds(0, 3)])
+        arrived(22 + 4 * b, fars[b].at[pl.ds(0, 3)])
         msgs[b][2] = total_of(fars[b], 4) * out_scale
-        to_plane(lambda p: msgs[b].at[2], lasts[b].at[plane_me], 21 + 4 * b)
+        to_plane(lambda p: msgs[b].at[2], lasts[b].at[plane_me], 23 + 4 * b)
         lasts[b][plane_me] = msgs[b][2]
 
     def finish_big(b):
-        arrived(21 + 4 * b, lasts[b].at[pl.ds(0, NP - 1)])
+        arrived(23 + 4 * b, lasts[b].at[pl.ds(0, NP - 1)])
         for p in range(NP):
             first = p * rows
             while first < (p + 1) * rows:
@@ -385,18 +463,18 @@
     def send_tiny_z():
         @pl.loop(1, Z)
         def _(s):
-            copy_to(tiny_ref.at[0], tinyz_ref.at[z_at], 26, z_device(lax.rem(z_at + s, Z))).start()
+            copy_to(tiny_ref.at[0], tinyz_ref.at[z_at], 29, z_device(lax.rem(z_at + s, Z))).start()
 
         tinyz_ref[z_at] = tiny_ref[0]
 
     def send_tiny_plane():
-        arrived(26, tinyz_ref.at[pl.ds(0, Z - 1)])
+        arrived(29, tinyz_ref.at[pl.ds(0, Z - 1)])
         tiny_ref[2] = total_of(tinyz_ref, Z)
-        to_plane(lambda p: tiny_ref.at[2], tinyp_ref.at[plane_me], 27)
+        to_plane(lambda p: tiny_ref.at[2], tinyp_ref.at[plane_me], 30)
         tinyp_ref[plane_me] = tiny_ref[2]
 
     def finish_tiny():
-        arrived(27, tinyp_ref.at[pl.ds(0, NP - 1)])
+        arrived(30, tinyp_ref.at[pl.ds(0, NP - 1)])
         put_tiny(0, total_of(tinyp_ref, NP) * out_scale)
 
     def gate_grad(b):
@@ -416,6 +494,14 @@
     def col_sum(x):
         return jnp.sum(x, axis=0, keepdims=True)
 
+    fetches[0].wait()
+    for i in range(R):
+        for j in range(R):
+            at = (i * R + j) * D
+            z_ref[0, at:at + D] = pair_ref[pl.ds(i * N + j, D, stride=R)]
+    fetches[2].wait()
+    fetches[3].wait()
+    fetches[5].wait()
     n0, r0 = normalise(z_ref[0])
     n_ref[0] = n0
     r_ref[0] = r0
@@ -423,14 +509,24 @@
     xt_ref[0, 0] = x0_split[0]
     xt_ref[0, 1] = x0_split[1]
     put_chunk(0, bias_rows(0, x0_split))
+    fetches[4].wait()
+    fetches[6].wait()
+    prepare(0)
     pl.semaphore_wait(barrier, D - 1 + NP - 1)
     gather_z(0)
-    prepare(0)
-    forward_near(0)
+    fetches[1].wait()
+    for i in range(R):
+        for j in range(R):
+            at = (i * R + j) * D
+            tile = grad_ref[pl.ds(i * N + j, D, stride=R)]
+            up_ref[at:at + D] = tile
+            put_stage(0, j * R + i, tile)
     project(0, x0_split)
-    forward_far(0)
+    forward(0)
     send_half(0, 0)
     prepare(1)
+    fetches[7].wait()
+    fetches[8].wait()
     gathered(0)
     for h in range(HEADS):
         bt_ref[0, h] = jnp.concatenate([gather_ref[0, :, i * HEADS + h, :] for i in range(R)], axis=0).T
@@ -452,17 +548,13 @@
     put_chunk(1, bias_rows(1, xm_split))
     gather_z(1)
     send_half(1, 1)
-    forward_near(1)
-    forward_far(1)
+    forward(1)
+
+    half_arrived(1, 0)
     send_half(0, 1)
-
-    half_arrived(1, 0)
     half_arrived(1, 1)
-
-    def columns_layout(x):
-        return jnp.concatenate([get_recv(x, i * R + j) for j in range(R) for i in range(R)], axis=0)
-
-    n1, r1 = normalise(columns_layout(1))
+    n1, r1 = normalise(
+        jnp.concatenate([get_recv(1, i * R + j) for j in range(R) for i in range(R)], axis=0))
     n_ref[1] = n1
     r_ref[1] = r1
     x1_split = split((n1 * gain_ref[1:2] + shift_ref[1:2]).T)
@@ -477,37 +569,34 @@
         for row in range(8):
             put_stage(slot, 8 * m + row, value[row * D:(row + 1) * D])
 
-    attend(1, 0, R)
-    u1 = update(1, 0, R)
-    stage_back(2, 0, u1[0:2 * N])
-    stage_back(2, 1, u1[2 * N:])
-    send_half(2, 0)
-
-    half_arrived(0, 0)
-    half_arrived(0, 1)
-    du1 = columns_layout(0)
-
-    def bias_grad_1():
-        for h in range(HEADS):
-            for i in range(R):
-                put_stage(4, i * HEADS + h, db_ref[1, h, i * D:(i + 1) * D])
-        reduce_y(0)
-
-    du1_split = backward(1, du1, bias_grad_1)
+    for m in range(2):
+        attend(1, 2 * m, 2 * m + 2)
+        stage_back(2, m, update(1, 2 * m, 2 * m + 2))
+
+    du1_halves = []
     for m in range(2):
         part = slice(2 * m * N, (2 * m + 2) * N)
+        half_arrived(0, m)
+        du1_halves.append(jnp.concatenate([get_recv(0, 8 * m + row) for row in range(8)], axis=0))
+        backward(1, split(du1_halves[m]), 2 * m, 2 * m + 2)
+        if m == 1:
+            for h in range(HEADS):
+                for i in range(R):
+                    put_stage(4, i * HEADS + h, db_ref[1, h, i * D:(i + 1) * D])
+            reduce_y()
         dx = dx_local(1, 2 * m, 2 * m + 2).T
         dx_ref[part] = dx
         stage_back(3, m, normalise_back(dx * gain_ref[1:2], n_ref[1, part], r_ref[1, part]))
         send_half(3, m)
-    reduce_z(0)
-    big_grads(1, (xt_ref[1, 0], xt_ref[1, 1]), du1_split)
+    reduce_z()
+    du1 = jnp.concatenate(du1_halves, axis=0)
+    big_grads(1, (xt_ref[1, 0], xt_ref[1, 1]), split(du1))
     send_big(1)
     tiny_ref[1, 0:1] = col_sum(dx_ref[...] * n_ref[1])
     tiny_ref[1, 1:2] = col_sum(dx_ref[...])
     tiny_ref[1, 6:7] = gate_grad(1)
     tiny_ref[1, 7:8] = col_sum(du1)
-    dxm_t, dbw1 = bias_part(1, reduced(0), (xt_ref[2, 0], xt_ref[2, 1]))
+    dxm_t, dbw1 = bias_part(1, reduced(), (xt_ref[2, 0], xt_ref[2, 1]))
     dxm = dxm_t.T
     tiny_ref[1, 0:1] += col_sum(dxm * nm_ref[...])
     tiny_ref[1, 1:2] += col_sum(dxm)
@@ -516,48 +605,50 @@
     send_near(1)
     half_arrived(3, 0)
     half_arrived(3, 1)
-    send_half(2, 1)
+    send_half(2, 0)
     for i in range(R):
         for j in range(R):
             at = (i * R + j) * D
             mg_ref[at:at + D] += get_recv(3, j * R + i)
 
-    def bias_grad_0():
-        for h in range(HEADS):
-            turned = db_ref[0, h].T
-            for i in range(R):
-                put_stage(5, i * HEADS + h, turned[i * D:(i + 1) * D])
-        reduce_y(1)
-
-    du0_split = backward(0, mg_ref[...], bias_grad_0)
+    du0_split = split(mg_ref[...])
+    backward(0, du0_split, 0, R)
+    for h in range(HEADS):
+        turned = db_ref[0, h].T
+        for i in range(R):
+            put_stage(5, i * HEADS + h, turned[i * D:(i + 1) * D])
+    swift_y()
     send_far(1)
     big_grads(0, (xt_ref[0, 0], xt_ref[0, 1]), du0_split)
-    reduce_z(1)
+    swift_z()
     send_big(0)
     tiny_ref[0, 6:7] = gate_grad(0)
     tiny_ref[0, 7:8] = col_sum(mg_ref[...])
     dxt_ref[...] = dx_local(0, 0, R)
-    half_arrived(2, 0)
-    half_arrived(2, 1)
-    for i in range(R):
-        for j in range(R):
-            at = (i * R + j) * D
-            new_ref[pl.ds(i * N + j, D, stride=R)] = z_ref[1, at:at + D] + get_recv(2, j * R + i)
     send_last(1)
     send_near(0)
-    dx0_t, dbw0 = bias_part(0, reduced(1), (xt_ref[0, 0], xt_ref[0, 1]))
+    dx0_t, dbw0 = bias_part(0, swift_reduced(), (xt_ref[0, 0], xt_ref[0, 1]))
     dx_ref[...] = (dxt_ref[...] + dx0_t).T
     tiny_ref[0, 0:1] = col_sum(dx_ref[...] * n_ref[0])
     tiny_ref[0, 1:2] = col_sum(dx_ref[...])
     tiny_ref[0, 2:2 + HEADS] = dbw0
     send_tiny_z()
+    send_half(2, 1)
     send_far(0)
     dz0 = normalise_back(dx_ref[...] * gain_ref[0:1], n_ref[0], r_ref[0])
     for i in range(R):
         for j in range(R):
             at = (i * R + j) * D
             igrad_ref[pl.ds(i * N + j, D, stride=R)] = mg_ref[at:at + D] + dz0[at:at + D]
+    stores[1].start()
     send_tiny_plane()
+    for j in range(R):
+        if j % 2 == 0:
+            half_arrived(2, j // 2)
+        for i in range(R):
+            at = (i * R + j) * D
+            new_ref[pl.ds(i * N + j, D, stride=R)] = z_ref[1, at:at + D] + get_recv(2, j * R + i)
+    stores[0].start()
     finish_big(1)
     tiny1 = last1_ref[0, rows:rows + 8]
     for p in range(1, NP):
@@ -567,14 +658,26 @@
     finish_tiny()
     finish_big(0)
 
+    for k in range(2, 9):
+        stores[k].start()
+
     for k, ref in sent:
         wait_bytes(ref, send_sem.at[k])
+    for store in stores:
+        store.wait()
 
 
 def copies(*refs):
-    count = len(refs) // 2
-    for k in range(count):
-        refs[count + k][...] = refs[k][...]
+    ins, outs, held, sems = refs[:9], refs[9:18], refs[18:27], refs[27]
+    fetches = [pltpu.make_async_copy(ins[k], held[k], sems.at[0, k]) for k in range(9)]
+    stores = [pltpu.make_async_copy(held[k], outs[k], sems.at[1, k]) for k in range(9)]
+    for fetch in fetches:
+        fetch.start()
+    for fetch, store in zip(fetches, stores):
+        fetch.wait()
+        store.start()
+    for store in stores:
+        store.wait()
 
 
 def body(D, NC, pair, pair_grad, gain, shift, w, bw, gs, wo, os):
@@ -582,15 +685,20 @@
     T = R * N
     NP = 2 * NC
     rows = 5 * C // NP
-    vmem = pl.BlockSpec(memory_space=pltpu.VMEM)
+    anywhere = pl.BlockSpec(memory_space=pl.ANY)
     out = lambda *shape: jax.ShapeDtypeStruct(shape, F32)
+    args = (pair.reshape(T, C), pair_grad.reshape(T, C), gain, shift, w, bw, gs, wo, os)
+    shapes_in = [out(*a.shape) for a in args]
+    shapes_out = [out(T, C), out(T, C), out(2, C), out(2, C), out(2, 4, C, C), out(2, HEADS, C), out(2, C),
+                  out(2, C, C), out(2, C)]
     results = pl.pallas_call(
         functools.partial(kernel, D, NC),
-        out_shape=[out(T, C), out(T, C), out(2, C), out(2, C), out(2, 4, C, C), out(2, HEADS, C), out(2, C),
-                   out(2, C, C), out(2, C)],
-        in_specs=[vmem] * 9,
-        out_specs=[vmem] * 9,
-        scratch_shapes=[
+        out_shape=shapes_out,
+        in_specs=[anywhere] * 9,
+        out_specs=[anywhere] * 9,
+        scratch_shapes=[pltpu.VMEM(s.shape, F32) for s in shapes_in + shapes_out] + [
+            pltpu.SemaphoreType.DMA((9,)),
+            pltpu.SemaphoreType.DMA((9,)),
             pltpu.VMEM((2, T, C), F32),
             pltpu.VMEM((2, T, C), F32),
             pltpu.VMEM((2, T, 1), F32),
@@ -617,6 +725,7 @@
             pltpu.VMEM((2, Z, R * R, C), F32),
             pltpu.VMEM((2, Z, R * R, C), F32),
             pltpu.VMEM((2, Z, R * R, C), F32),
+            pltpu.VMEM((10, R * R, C), F32),
             pltpu.VMEM((2, NP, rows, C), F32),
             pltpu.VMEM((2, NP, rows, C), F32),
             pltpu.VMEM((3, rows, C), F32),
@@ -630,18 +739,19 @@
             pltpu.VMEM((3, 8, C), F32),
             pltpu.VMEM((Z, 8, C), F32),
             pltpu.VMEM((NP, 8, C), F32),
-            pltpu.SemaphoreType.DMA((28,)),
-            pltpu.SemaphoreType.DMA((28,)),
+            pltpu.SemaphoreType.DMA((31,)),
+            pltpu.SemaphoreType.DMA((31,)),
         ],
         compiler_params=pltpu.CompilerParams(
             collective_id=0, has_side_effects=True, vmem_limit_bytes=56 * 1024 * 1024),
-    )(pair.reshape(T, C), pair_grad.reshape(T, C), gain, shift, w, bw, gs, wo, os)
+    )(*args)
     results = pl.pallas_call(
         copies,
-        out_shape=[jax.ShapeDtypeStruct(r.shape, F32) for r in results],
-        in_specs=[vmem] * 9,
-        out_specs=[vmem] * 9,
-        compiler_params=pltpu.CompilerParams(vmem_limit_bytes=16 * 1024 * 1024),
+        out_shape=shapes_out,
+        in_specs=[anywhere] * 9,
+        out_specs=[anywhere] * 9,
+        scratch_shapes=[pltpu.VMEM(s.shape, F32) for s in shapes_out] + [pltpu.SemaphoreType.DMA((2, 9))],
+        compiler_params=pltpu.CompilerParams(vmem_limit_bytes=56 * 1024 * 1024),
     )(*results)
     return (results[0].reshape(pair.shape), results[1].reshape(pair.shape)) + tuple(results[2:])
 

time: 133 us -> 127 us (0.955)
  local copies, waits for them, and re-layouts: 4.52 us -> 0 us
    unnamed x18 -> x0, local copies, waits for them, and re-layouts: 4.52 us -> none
where the time goes in v3:
time: 127 us
  Pallas kernels  126 us (99%)
    pallas_call x1, Pallas kernels, body(): pl.pallas_call(functools.partial(kernel, D, NC), out_shape=shapes_out, in...  124 us

profile of v3, /device:TPU:1, one launch (start us, length us, event | category | flops | bytes accessed | tf_op | source)
XLA Modules:
  0.0 127.2 jit_solution(7823739122191891796)
XLA Ops:
  0.6 124.2 %shard_map.160 = (f32[512,128]{1,0:T(8,128)}, f32[512,128]{1,0:T(8,128)}, f32[2,128]{1,0:T(2,128)}, f32[2,128]{1,0:T(2,128)}, f32[2,4,128,128]{3,2,1,0:T(8,128)}...) custom-call(f32[512,128]{1,0:T(8,128)} %bitcast.4, f32[512,128]{1,0:T(8,128)} %bitcast.5, ...), custom_call_target="tpu_custom_call" | custom-call | tf_op jit(solution)/shard_map/pallas_call | solution.py:694
  124.9 2.2 %shard_map.161 = (f32[512,128]{1,0:T(8,128)}, f32[512,128]{1,0:T(8,128)}, f32[2,128]{1,0:T(2,128)}, f32[2,128]{1,0:T(2,128)}, f32[2,4,128,128]{3,2,1,0:T(8,128)}...) custom-call(f32[512,128]{1,0:T(8,128)} %get-tuple-element.27.refs_0_, ...), custom_call_target="tpu_custom_call" | custom-call | tf_op jit(solution)/shard_map/pallas_call | solution.py:748

commit v4 on v3

--- a/solution.py
+++ b/solution.py
@@ -74,7 +74,7 @@
     wt_ref, xt_ref, pt_ref, at_ref, ot_ref, yt_ref, dot_ref, dpt_ref, bt_ref, db_ref,
     stage_ref, chunk_ref, recv_ref, gather_ref, pairsum_ref, zstage_ref, zrecv_ref, direct_ref,
     big_ref, bigr_ref, msg0_ref, msg1_ref, near0_ref, near1_ref, far0_ref, far1_ref, last0_ref, last1_ref,
-    tiny_ref, tinyz_ref, tinyp_ref,
+    tiny_ref, tinyz_ref, tinyp_ref, column_ref,
     send_sem, recv_sem,
 ):
     pair_ref, grad_ref, gain_ref, shift_ref, w_ref, bw_ref, gs_ref, wo_ref, os_ref = held
@@ -433,9 +433,29 @@
 
         fars[b][block] = msgs[b][1]
 
+    def send_z(b):
+        arrived(20 + 4 * b, bigr_ref.at[b, pl.ds(0, NP - 1)])
+        msgs[b][0] = total_of(bigr_ref.at[b], NP)
+
+        def to(s):
+            copy_to(msgs[b].at[0], column_ref.at[z_at], 21 + 4 * b, z_device(lax.rem(z_at + s, Z))).start()
+
+        to(8)
+
+        @pl.loop(1, 8)
+        def _(s):
+            to(8 - s)
+            to(8 + s)
+
+        column_ref[z_at] = msgs[b][0]
+
     def send_last(b):
-        arrived(22 + 4 * b, fars[b].at[pl.ds(0, 3)])
-        msgs[b][2] = total_of(fars[b], 4) * out_scale
+        if b == 0:
+            arrived(21, column_ref.at[pl.ds(0, Z - 1)])
+            msgs[b][2] = total_of(column_ref, Z) * out_scale
+        else:
+            arrived(22 + 4 * b, fars[b].at[pl.ds(0, 3)])
+            msgs[b][2] = total_of(fars[b], 4) * out_scale
         to_plane(lambda p: msgs[b].at[2], lasts[b].at[plane_me], 23 + 4 * b)
         lasts[b][plane_me] = msgs[b][2]
 
@@ -625,8 +645,7 @@
     tiny_ref[0, 6:7] = gate_grad(0)
     tiny_ref[0, 7:8] = col_sum(mg_ref[...])
     dxt_ref[...] = dx_local(0, 0, R)
-    send_last(1)
-    send_near(0)
+    send_z(0)
     dx0_t, dbw0 = bias_part(0, swift_reduced(), (xt_ref[0, 0], xt_ref[0, 1]))
     dx_ref[...] = (dxt_ref[...] + dx0_t).T
     tiny_ref[0, 0:1] = col_sum(dx_ref[...] * n_ref[0])
@@ -634,7 +653,6 @@
     tiny_ref[0, 2:2 + HEADS] = dbw0
     send_tiny_z()
     send_half(2, 1)
-    send_far(0)
     dz0 = normalise_back(dx_ref[...] * gain_ref[0:1], n_ref[0], r_ref[0])
     for i in range(R):
         for j in range(R):
@@ -642,6 +660,8 @@
             igrad_ref[pl.ds(i * N + j, D, stride=R)] = mg_ref[at:at + D] + dz0[at:at + D]
     stores[1].start()
     send_tiny_plane()
+    send_last(0)
+    send_last(1)
     for j in range(R):
         if j % 2 == 0:
             half_arrived(2, j // 2)
@@ -654,7 +674,6 @@
     for p in range(1, NP):
         tiny1 = tiny1 + last1_ref[p, rows:rows + 8]
     put_tiny(1, tiny1)
-    send_last(0)
     finish_tiny()
     finish_big(0)
 
@@ -739,6 +758,7 @@
             pltpu.VMEM((3, 8, C), F32),
             pltpu.VMEM((Z, 8, C), F32),
             pltpu.VMEM((NP, 8, C), F32),
+            pltpu.VMEM((Z, rows, C), F32),
             pltpu.SemaphoreType.DMA((31,)),
             pltpu.SemaphoreType.DMA((31,)),
         ],

time: 127 us -> 135 us (1.063)
  Pallas kernels: 126 us -> 134 us
    pallas_call x1, Pallas kernels: 124 us -> 131 us  [body(): pl.pallas_call(functools.partial(kernel, D, NC), out_shape=shapes_out, in...]
where the time goes in v4:
time: 135 us; the launch traced here: 134 us
  Pallas kernels  134 us (99%)
    pallas_call x1, Pallas kernels, body(): pl.pallas_call(functools.partial(kernel, D, NC), out_shape=shapes_out, in...  131 us

profile of v4, /device:TPU:1, one launch (start us, length us, event | category | flops | bytes accessed | tf_op | source)
XLA Modules:
  0.0 134.4 jit_solution(14128856050998105227)
XLA Ops:
  0.6 131.4 %shard_map.160 = (f32[512,128]{1,0:T(8,128)}, f32[512,128]{1,0:T(8,128)}, f32[2,128]{1,0:T(2,128)}, f32[2,128]{1,0:T(2,128)}, f32[2,4,128,128]{3,2,1,0:T(8,128)}...) custom-call(f32[512,128]{1,0:T(8,128)} %bitcast.4, f32[512,128]{1,0:T(8,128)} %bitcast.5, ...), custom_call_target="tpu_custom_call" | custom-call | tf_op jit(solution)/shard_map/pallas_call | solution.py:713
  132.1 2.2 %shard_map.161 = (f32[512,128]{1,0:T(8,128)}, f32[512,128]{1,0:T(8,128)}, f32[2,128]{1,0:T(2,128)}, f32[2,128]{1,0:T(2,128)}, f32[2,4,128,128]{3,2,1,0:T(8,128)}...) custom-call(f32[512,128]{1,0:T(8,128)} %get-tuple-element.27.refs_0_, ...), custom_call_target="tpu_custom_call" | custom-call | tf_op jit(solution)/shard_map/pallas_call | solution.py:768
